TPU v7x, 32 devices: a whole 2x2x4 slice. The times are simulated.
32 devices in a mesh: gy: 8 (over z, y), gz: 4 (over x, core).
Axes of the slice: x: 2, y: 2, z: 4, core: 2. Of those that a mesh axis runs over, the one named last changes fastest.
Arguments:
- field: bfloat16 [32, 8, 128, 1024], P(None, None, 'gy', 'gz'), may hold values from -6 to 6
- spectral_weight: bfloat16 [256, 32, 1024], P('gy', 'gz'), may hold values from -1 to 1
- point_weight: bfloat16 [32, 32], replicated, may hold values from -1 to 1
- bias: float32 [32], replicated, may hold values from -3 to 3
Outputs:
- layer_out: bfloat16 [32, 8, 128, 1024], P(None, None, 'gy', 'gz')
All inputs are finite; a program needn't handle non-finite values.
Results may differ from a plain program's by a relative error of at most 0.013.
Values may be sent and summed in bfloat16 or wider, within the bound.
A program may use at most 64 MiB of HBM per device.

v0:
```python
import math

import jax
import jax.numpy as jnp
from jax import lax
from jax.sharding import PartitionSpec as P

KY = 32
KZ = 32


def basis(count, length, start, size, norm):
    modes = jnp.arange(count, dtype=jnp.float32)[:, None]
    spots = (start + lax.iota(jnp.int32, size)).astype(jnp.float32)[None, :]
    value = norm * jnp.cos(jnp.pi * modes * (spots + 0.5) / length)
    return jnp.where(modes == 0, value * math.sqrt(0.5), value)


def shards(field, spectral_weight, point_weight, bias):
    highest = lax.Precision.HIGHEST
    chans, planes, rows, depth = field.shape
    rows_devs = lax.axis_size("gy")
    depth_devs = lax.axis_size("gz")
    total_rows = rows * rows_devs
    total_depth = depth * depth_devs
    row_start = lax.axis_index("gy") * rows
    depth_start = lax.axis_index("gz") * depth
    analysis_z = basis(KZ, total_depth, depth_start, depth, math.sqrt(2.0 / total_depth)).astype(
        jnp.bfloat16
    )
    analysis_y = basis(KY, total_rows, row_start, rows, math.sqrt(2.0 / total_rows))
    analysis_x = basis(planes, planes, 0, planes, math.sqrt(2.0 / planes))
    first_share = planes * KY // rows_devs
    depth_share = KZ // depth_devs
    weight = spectral_weight.reshape(first_share, depth_share, chans, chans).astype(jnp.float32)
    projected = jnp.einsum("cxyz,kz->cxyk", field, analysis_z, preferred_element_type=jnp.float32)
    partial_value = jnp.einsum("cxyk,jy->cxjk", projected, analysis_y, precision=highest)
    partial_value = jnp.einsum("cxjk,ix->cijk", partial_value, analysis_x, precision=highest)
    partial_value = partial_value.reshape(chans, planes * KY, KZ)
    reduced = lax.psum_scatter(partial_value, "gy", scatter_dimension=1, tiled=True)
    owned = lax.psum_scatter(reduced, "gz", scatter_dimension=2, tiled=True)
    mixed = jnp.einsum("cab,abco->oab", owned, weight, precision=highest).astype(jnp.bfloat16)
    widened = lax.all_gather(mixed, "gz", axis=2, tiled=True)
    full_modes = lax.all_gather(widened, "gy", axis=1, tiled=True)
    modes = full_modes.astype(jnp.float32).reshape(chans, planes, KY, KZ)
    synth_x = basis(planes, planes, 0, planes, math.sqrt(2.0 / planes))
    synth_y = basis(KY, total_rows, row_start, rows, math.sqrt(2.0 / KY))
    synth_z = basis(KZ, total_depth, depth_start, depth, math.sqrt(2.0 / KZ))
    spatial = jnp.einsum("cijk,ix->cxjk", modes, synth_x, precision=highest)
    spatial = jnp.einsum("cxjk,jy->cxyk", spatial, synth_y, precision=highest)
    spatial = jnp.einsum("cxyk,kz->cxyz", spatial, synth_z, precision=highest)
    local = jnp.einsum("cxyz,co->oxyz", field, point_weight, preferred_element_type=jnp.float32)
    total = spatial + local + bias[:, None, None, None]
    return jax.nn.gelu(total, approximate=True).astype(jnp.bfloat16)


def solution(mesh):
    return jax.shard_map(
        shards,
        mesh=mesh,
        in_specs=(P(None, None, "gy", "gz"), P("gy", "gz", None), P(), P()),
        out_specs=P(None, None, "gy", "gz"),
        check_vma=False,
    )
```

profile of v0, /device:TPU:1, one launch (start us, length us, event | category | flops | bytes accessed | tf_op | source)
XLA Modules:
  0.0 200.2 jit_solution(13649701607990245929)
XLA Ops:
  6.5 0.0 copy-start
  6.5 0.0 reduce-scatter.7.cloned.1.call-start
  6.6 1.5 copy-done
  8.1 3.2 %fusion.22 = f32[32,8,16,32]{0,3,2,1:T(8,128)} fusion(bf16[32,8,16,256]{3,2,1,0:T(8,128)(2,1)S(1)} %copy-done, f32[256]{0:T(256)S(1)} %convert_add_fusion, f32[32]{0:T(128)S(1)} %iota_multiply_fusion.1, pred[32]{0:T(512)(128)(4,1)S(1)} %iota_compare_fusion.1), kind=kOutput, calls=%fused_computation.25 | convolution fusion | flops 67158016 | bytes 2622624 | tf_op jit(solution)/shard_map/cxyz,kz->cxyk/dot_general | solution.py:36
  11.3 3.7 %copy.33 = f32[32,8,16,32]{3,2,1,0:T(8,128)} copy(f32[32,8,16,32]{0,3,2,1:T(8,128)} %fusion.22) | data formatting | bytes 1048576 | tf_op jit(solution)/shard_map/cxyz,kz->cxyk/dot_general | solution.py:36
  15.0 5.3 %convolution_bitcast_fusion.1 = f32[32,8,32,32]{3,2,1,0:T(8,128)S(1)} fusion(f32[32,8,16,32]{3,2,1,0:T(8,128)} %copy.33, f32[16]{0:T(128)S(1)} %convert_add_fusion.2, f32[32]{0:T(128)S(1)} %iota_multiply_fusion.1, pred[32]{0:T(512)(128)(4,1)S(1)} %iota_compare_fusion.1), kind=kOutput, calls=%fused_computation.18 | convolution fusion | flops 50334208 | bytes 1573088 | tf_op jit(solution)/shard_map/cxyk,jy->cxjk/dot_general | solution.py:37
  20.3 5.9 %fusion.13 = f32[32,8,32,32]{3,1,2,0:T(8,128)S(1)} fusion(f32[32,8,32,32]{3,2,1,0:T(8,128)S(1)} %convolution_bitcast_fusion.1, f32[8]{0:T(128)S(1)} %get-tuple-element.5, f32[8]{0:T(128)S(1)} %get-tuple-element.6, pred[8]{0:T(512)(128)(4,1)S(1)} %iota_compare_fusion), kind=kOutput, calls=%fused_computation.16 | convolution fusion | flops 25166144 | bytes 2097224 | tf_op jit(solution)/shard_map/cxjk,ix->cijk/dot_general | solution.py:38
  26.2 4.6 %copy.62 = f32[32,8,32,32]{3,0,2,1:T(8,128)} copy(f32[32,8,32,32]{3,1,2,0:T(8,128)S(1)} %fusion.13) | data formatting | bytes 2097152
  30.8 0.0 copy-start.2
  30.8 4.6 %reshape.62 = f32[256,1024]{1,0:T(8,128)} reshape(f32[256,32,32]{2,1,0:T(8,128)} %bitcast.53) | data formatting | bytes 2097152
  35.5 0.0 copy-start.3
  35.5 0.0 reduce-scatter.7.cloned.1.call-update
  35.5 0.0 reduce-scatter.5.cloned.1.call-start
  35.6 0.0 copy-done.2
  35.6 2.6 %reshape.51 = bf16[32,8,32,32]{3,2,1,0:T(8,128)(2,1)} reshape(bf16[32,8,1024]{2,1,0:T(8,128)(2,1)S(1)} %copy-done.2) | data formatting | bytes 1048576 | tf_op jit(solution)/shard_map/reshape | solution.py:35
  38.1 61.6 %reduce-scatter.7.cloned.1.call-done = f32[32,1024]{1,0:T(8,128)} async-done(((f32[256,1024]{1,0:T(8,128)}), f32[32,1024]{1,0:T(8,128)}) %reduce-scatter.7.cloned.1.call-update) | async-done | bytes 131088
  99.7 1.1 reshape.63
  100.8 1.1 copy.61
  101.9 0.0 reduce-scatter.5.cloned.1.call-update
  101.9 0.0 copy-done.3
  101.9 3.3 %fusion.18 = f32[32,8,16,256]{3,0,2,1:T(8,128)} fusion(bf16[32,8,16,256]{3,2,1,0:T(8,128)(2,1)S(1)} %copy-done, bf16[32,32]{1,0:T(8,128)(2,1)S(1)} %copy-done.3), kind=kOutput, calls=%fused_computation.21 | convolution fusion | flops 67108864 | bytes 6293504 | tf_op jit(solution)/shard_map/cxyz,co->oxyz/dot_general | solution.py:52
  105.2 19.4 %reduce-scatter.5.cloned.1.call-done = f32[32,32,8]{1,2,0:T(8,128)} async-done(((f32[32,32,32]{1,2,0:T(8,128)}), f32[32,32,8]{1,2,0:T(8,128)}) %reduce-scatter.5.cloned.1.call-update) | async-done | bytes 32784 | tf_op jit(solution)/shard_map/reduce_scatter | solution.py:41
  124.6 1.0 copy.64
  125.6 2.6 %multiply_reduce_fusion = bf16[32,8,32]{2,1,0:T(8,128)(2,1)S(1)} fusion(bf16[32,8,32,32]{3,2,1,0:T(8,128)(2,1)} %reshape.51, f32[32,8,32]{2,1,0:T(8,128)S(1)} %copy.64), kind=kLoop, calls=%fused_computation.9 | loop fusion | flops 778240 | bytes 573440
  128.3 0.1 copy.51
  128.4 6.3 %all_gather.6 = bf16[32,32,32]{1,0,2:T(8,128)(2,1)S(1)} all-gather(bf16[32,32,8]{1,0,2:T(8,128)(2,1)S(1)} %bitcast.56), channel_id=1, replica_groups=mesh['gy'=8,'gz'=4] {'gz'}, dimensions={2}, use_global_device_ids=true | all-gather | bytes 81920 | tf_op jit(solution)/shard_map/all_gather | solution.py:43
  134.7 0.6 copy.37
  135.2 43.9 %all_gather.7 = bf16[32,256,32]{2,0,1:T(8,128)(2,1)S(1)} all-gather(bf16[32,32,32]{2,0,1:T(8,128)(2,1)S(1)} %copy.37), channel_id=1, replica_groups=mesh['gy'=8,'gz'=4] {'gy'}, dimensions={1}, use_global_device_ids=true | all-gather | bytes 589824 | tf_op jit(solution)/shard_map/all_gather | solution.py:44
  179.2 4.0 %convolution_bitcast_fusion = f32[32,8,32,32]{3,1,2,0:T(8,128)S(1)} fusion(bf16[32,8,32,32]{3,0,2,1:T(8,128)(2,1)S(1)} %bitcast.54, f32[8]{0:T(128)S(1)} %get-tuple-element.5, f32[8]{0:T(128)S(1)} %get-tuple-element.6, pred[8]{0:T(512)(128)(4,1)S(1)} %iota_compare_fusion), kind=kOutput, calls=%fused_computation.17 | convolution fusion | flops 25166144 | bytes 1572936 | tf_op jit(solution)/shard_map/cijk,ix->cxjk/dot_general | solution.py:49
  183.2 0.0 copy-start.1
  183.2 0.0 copy-start.4
  183.2 2.7 %fusion.9 = f32[16,32,8,32]{3,0,2,1:T(8,128)S(1)} fusion(f32[32,8,32,32]{3,1,2,0:T(8,128)S(1)} %convolution_bitcast_fusion, f32[16]{0:T(128)S(1)} %convert_add_fusion.2, f32[32]{0:T(128)S(1)} %iota_multiply_fusion.1, pred[32]{0:T(512)(128)(4,1)S(1)} %iota_compare_fusion.1), kind=kOutput, calls=%fused_computation.12 | convolution fusion | flops 50334208 | bytes 1573088 | tf_op jit(solution)/shard_map/cxjk,jy->cxyk/dot_general | solution.py:50
  185.9 0.0 copy-done.1
  185.9 0.0 copy-done.4
  185.9 7.5 %fusion.7 = bf16[32,8,16,256]{3,2,1,0:T(8,128)(2,1)} fusion(f32[32,8,16,256]{3,0,2,1:T(8,128)S(1)} %copy-done.1, f32[16,32,8,32]{3,0,2,1:T(8,128)S(1)} %fusion.9, f32[32]{0:T(128)S(1)} %copy-done.4, f32[256]{0:T(256)S(1)} %convert_add_fusion, f32[32]{0:T(128)S(1)} %iota_multiply_fusion.1, pred[32]{0:T(512)(128)(4,1)S(1)} %iota_compare_fusion.1), kind=kOutput, calls=%fused_computation.8 | convolution fusion | flops 414228480 | bytes 6817056 | tf_op jit(solution)/shard_map/cxyk,kz->cxyz/dot_general | solution.py:51
  (6 shorter events, 0.0 us)
Async XLA Ops:
  6.5 1.6 copy-start
  6.5 93.1 %reduce-scatter.7.cloned.1.call-start = ((), (), s32[]{:S(2)}) async-start(), calls=%async_computation.3 | async-start | bytes 1179648
  30.8 4.7 %copy-start.2 = (bf16[32,8,1024]{2,1,0:T(8,128)(2,1)S(1)}, bf16[32,8,1024]{2,1,0:T(8,128)(2,1)}, u32[]{:S(2)}) copy-start(bf16[32,8,1024]{2,1,0:T(8,128)(2,1)} %param.5) | copy-start | bytes 1572868
  35.5 66.4 %copy-start.3 = (bf16[32,32]{1,0:T(8,128)(2,1)S(1)}, bf16[32,32]{1,0:T(8,128)(2,1)}, u32[]{:S(2)}) copy-start(bf16[32,32]{1,0:T(8,128)(2,1)} %param.6) | copy-start | bytes 6148
  35.5 89.1 %reduce-scatter.5.cloned.1.call-start = ((), (), s32[]{:S(2)}) async-start(), calls=%async_computation.2 | async-start | bytes 655360 | tf_op jit(solution)/shard_map/reduce_scatter | solution.py:41
  183.2 2.8 %copy-start.1 = (f32[32,8,16,256]{3,0,2,1:T(8,128)S(1)}, f32[32,8,16,256]{3,0,2,1:T(8,128)}, u32[]{:S(2)}) copy-start(f32[32,8,16,256]{3,0,2,1:T(8,128)} %fusion.18) | copy-start | bytes 12582916
  183.2 2.8 %copy-start.4 = (f32[32]{0:T(128)S(1)}, f32[32]{0:T(128)}, u32[]{:S(2)}) copy-start(f32[32]{0:T(128)} %param.7) | copy-start | bytes 388
Sparse Core Ops, SparseCore 0:
  35.6 64.0 reduce-scatter.6
  102.3 22.2 reduce-scatter.4
where the time goes:
time: 202 us; the launch traced here: 200 us
  waiting for transfers between devices  81 us (40%)
  blocking collectives  50.2 us (25%)
  matrix products  31.9 us (16%)
  local copies, waits for them, and re-layouts  20.9 us (10%)
  between operations  13.6 us (7%)
  other arithmetic  2.69 us (1%)
    unnamed x3, waiting for transfers between devices  61.6 us
    all_gather x1, blocking collectives, shards(): full_modes = lax.all_gather(widened, 'gy', axis=1, tiled=True)  43.9 us
    reduce_scatter x1, waiting for transfers between devices, shards(): owned = lax.psum_scatter(reduced, 'gz', scatter_dimension=2, tiled=True)  19.4 us
    unnamed x15, local copies, waits for them, and re-layouts  14 us
    dot_general x1, matrix products, shards(): spatial = jnp.einsum('cxyk,kz->cxyz', spatial, synth_z, precision=highest)  7.46 us
    all_gather x1, blocking collectives, shards(): widened = lax.all_gather(mixed, 'gz', axis=2, tiled=True)  6.3 us
    dot_general x1, matrix products, shards(): jnp.einsum('cxjk,ix->cijk', partial_value, analysis_x, precision=highest)  5.91 us
    dot_general x1, matrix products, shards(): jnp.einsum('cxyk,jy->cxjk', projected, analysis_y, precision=highest)  5.3 us
  transfers between devices with their start and end apart: 2, of which 2 were waited for; matrix products, arithmetic and copies ran while one was open for 3% of the time, Pallas kernels for 0%

commit v1 on v0

v1 whole, which is shorter than its diff:
```python
import functools
import math

import jax
import jax.numpy as jnp
import ml_dtypes
import numpy as np
from jax import lax
from jax.experimental import pallas as pl
from jax.experimental.pallas import tpu as pltpu
from jax.sharding import PartitionSpec as P

KY = 32
KZ = 32
BF16 = jnp.bfloat16
F32 = jnp.float32
MESH = pl.DeviceIdType.MESH
SHARE = 8
HALF = 256


def basis(count, length, norm):
    modes = np.arange(count)[:, None]
    spots = np.arange(length)[None, :]
    value = norm * np.cos(np.pi * modes * (spots + 0.5) / length)
    return np.where(modes == 0, value * math.sqrt(0.5), value)


def tables(n_y, n_z, planes, rows, depth, first_share):
    total_rows, total_depth = rows * n_y, depth * n_z
    az = basis(KZ, total_depth, math.sqrt(2.0 / total_depth))
    az = az.astype(np.float32).astype(ml_dtypes.bfloat16).astype(np.float64)
    ax = basis(planes, planes, math.sqrt(2.0 / planes))
    sz = basis(KZ, total_depth, math.sqrt(2.0 / KZ))

    def joint(x_basis, z_basis):
        z = z_basis.reshape(n_z, SHARE, n_z, depth)
        both = np.einsum("ix,bkdz->dxbikz", x_basis, z)
        return both.reshape(n_z, planes, planes * KZ, depth).astype(ml_dtypes.bfloat16)

    ay = basis(KY, total_rows, math.sqrt(2.0 / total_rows))
    sy = basis(KY, total_rows, math.sqrt(2.0 / KY))
    blocks = KY // first_share

    def lanes(y_basis):
        parts = y_basis.reshape(blocks, first_share, n_y, rows)
        return np.tile(parts, (1, 1, 1, HALF // rows)).astype(np.float32)

    analysis_y = lanes(ay)
    synth_y = np.ascontiguousarray(np.swapaxes(lanes(sy), 1, 2))
    return joint(ax, az), joint(ax, sz), analysis_y, synth_y


def select(rows, columns, row_of, column_of):
    r = lax.broadcasted_iota(jnp.int32, (rows, columns), 0)
    c = lax.broadcasted_iota(jnp.int32, (rows, columns), 1)
    return jnp.where(row_of(r) == column_of(c), 1.0, 0.0).astype(F32)


def spectral_kernel(
    n_y, n_z, field, a_tab, weight, point, ay_tab, sy_tab, gt_out, kron_out,
    f_v, a_v, w_v, ay_v, sy_v, e1, e2, part, got1, owned, got2, u_v, m_v, tout, got3, modes,
    load_sem, send1, recv1, send2, recv2, send3, recv3, send4, recv4,
):
    me_y, me_z = lax.axis_index("gy"), lax.axis_index("gz")
    planes = f_v.shape[1]
    chans = f_v.shape[0]
    rows = f_v.shape[2]
    group = n_y // planes
    first_share = w_v.shape[0]
    mine, place = lax.div(me_y, group), lax.rem(me_y, group)
    block = place if first_share < KY else 0
    others = [(d, t) for d in range(planes) for t in range(group)][1:]

    def at(d, t):
        return lax.rem(mine + d, planes) * group + lax.rem(place + t, group)

    def came(d, t):
        return lax.rem(mine - d + planes, planes) * group + lax.rem(place - t + group, group)

    def peer(e):
        return lax.rem(me_z + e, n_z)

    barrier = pltpu.get_barrier_semaphore()
    for e in range(1, n_z):
        pl.semaphore_signal(
            barrier, inc=1, device_id=(me_y, peer(e)), device_id_type=MESH
        )
    for d, t in others:
        pl.semaphore_signal(
            barrier, inc=1, device_id=(at(d, t), me_z), device_id_type=MESH
        )

    half = chans // 2
    loads = [
        pltpu.make_async_copy(field.at[0:half], f_v.at[0:half], load_sem.at[0]),
        pltpu.make_async_copy(a_tab.at[me_z], a_v, load_sem.at[1]),
        pltpu.make_async_copy(field.at[half:chans], f_v.at[half:chans], load_sem.at[2]),
        pltpu.make_async_copy(weight, w_v, load_sem.at[3]),
        pltpu.make_async_copy(ay_tab.at[block], ay_v, load_sem.at[4]),
        pltpu.make_async_copy(sy_tab.at[block], sy_v, load_sem.at[5]),
    ]
    for load in loads:
        load.start()

    halves = []
    loads[1].wait()
    for h in range(2):
        loads[2 * h].wait()
        total = jnp.zeros((planes * KZ, HALF), F32)
        for x in range(planes):
            grid = f_v[h * half:(h + 1) * half, x].reshape(HALF, f_v.shape[3])
            total += lax.dot_general(
                a_v[x], grid, (((1,), (1,)), ((), ())), preferred_element_type=F32
            )
        halves.append(total.reshape(planes * n_z, SHARE, HALF))
    part[...] = jnp.concatenate(halves, axis=1).astype(BF16)

    pl.semaphore_wait(barrier, n_z - 1 + len(others))

    started = []
    order = list(range(1, planes)) + [0]
    first = {}
    for d in order:
        i = lax.rem(mine + d, planes)
        for e in range(1, n_z):
            copy = pltpu.make_async_remote_copy(
                src_ref=part.at[peer(e) * planes + i],
                dst_ref=got1.at[e - 1, i],
                send_sem=send1.at[e - 1, d],
                recv_sem=recv1.at[e - 1, d],
                device_id=(me_y, peer(e)),
                device_id_type=MESH,
            )
            copy.start()
            first[e, d] = copy
            started.append(copy)

    e1[...] = select(*e1.shape, lambda r: r // rows, lambda c: c // chans).astype(BF16)
    e2[...] = select(*e2.shape, lambda r: r % chans, lambda c: c // rows).astype(BF16)

    second = {}
    for d in order:
        i = lax.rem(mine + d, planes)
        total = part[me_z * planes + i].astype(F32)
        for e in range(1, n_z):
            first[e, d].wait_recv()
            total += got1[e - 1, i].astype(F32)
        owned[i] = total.astype(BF16)
        for t in range(group):
            if d == 0 and t == 0:
                got2[me_y] = total.astype(BF16)
                continue
            copy = pltpu.make_async_remote_copy(
                src_ref=owned.at[i],
                dst_ref=got2.at[me_y],
                send_sem=send2.at[d * group + t],
                recv_sem=recv2.at[d * group + t],
                device_id=(at(d, t), me_z),
                device_id_type=MESH,
            )
            copy.start()
            second[d, t] = copy
            started.append(copy)

    spread = select(chans * rows, chans, lambda r: r // rows, lambda c: c).astype(BF16)
    wide = lax.dot_general(
        spread, point[...], (((1,), (1,)), ((), ())), preferred_element_type=F32
    ).astype(BF16)
    wide = lax.dot_general(
        wide, spread, (((1,), (1,)), ((), ())), preferred_element_type=F32
    )
    same = select(*wide.shape, lambda r: r % rows, lambda c: c % rows)
    kron_out[...] = (wide * same).astype(BF16)

    for load in loads[3:]:
        load.wait()
    for d, t in others:
        second[d, t].wait_recv()
    for h in range(2):
        pieces = [got2[s].astype(F32)[h * SHARE:(h + 1) * SHARE] for s in range(n_y)]
        for j in range(first_share):
            total = pieces[0] * ay_v[j, 0:1, :]
            for s in range(1, n_y):
                total += pieces[s] * ay_v[j, s:s + 1, :]
            u_v[j, :, h * HALF:(h + 1) * HALF] = total

    mode_rows = first_share * SHARE
    spectrum = jnp.dot(
        u_v[...].reshape(mode_rows, 2 * HALF).astype(BF16), e1[...], preferred_element_type=F32
    )
    terms = spectrum * w_v[...].astype(F32).reshape(mode_rows, chans * chans)
    mixed = jnp.dot(terms.astype(BF16), e2[...], preferred_element_type=F32)
    m_v[...] = mixed.reshape(first_share, SHARE, 2 * HALF)

    third = {}
    for d, t in others + [(0, 0)]:
        target = at(d, t)
        synth = sy_v[target]
        sides = []
        for h in range(2):
            total = m_v[0, :, h * HALF:(h + 1) * HALF] * synth[0:1, :]
            for j in range(1, first_share):
                total += m_v[j, :, h * HALF:(h + 1) * HALF] * synth[j:j + 1, :]
            sides.append(total)
        value = jnp.concatenate(sides, axis=0).astype(BF16)
        if d == 0 and t == 0:
            got3[me_y] = value
            continue
        tout[target] = value
        copy = pltpu.make_async_remote_copy(
            src_ref=tout.at[target],
            dst_ref=got3.at[me_y],
            send_sem=send3.at[d * group + t],
            recv_sem=recv3.at[d * group + t],
            device_id=(target, me_z),
            device_id_type=MESH,
        )
        copy.start()
        third[d, t] = copy
        started.append(copy)

    fourth = []
    for d in range(planes):
        i = lax.rem(mine - d + planes, planes)
        total = None
        for t in range(group):
            if (d, t) != (0, 0):
                third[d, t].wait_recv()
            piece = got3[came(d, t)]
            if group > 1:
                piece = piece.astype(F32)
            total = piece if total is None else total + piece
        slot = me_z * planes + i
        modes[slot] = total.astype(BF16)
        for e in range(1, n_z):
            copy = pltpu.make_async_remote_copy(
                src_ref=modes.at[slot],
                dst_ref=modes.at[slot],
                send_sem=send4.at[e - 1, d],
                recv_sem=recv4.at[e - 1, d],
                device_id=(me_y, peer(e)),
                device_id_type=MESH,
            )
            copy.start()
            fourth.append(copy)
    for copy in fourth:
        copy.wait_recv()
    for h in range(2):
        value = modes[...].astype(F32)[:, h * SHARE:(h + 1) * SHARE, :]
        value = value.reshape(planes * KZ, HALF)
        gt_out[h * HALF:(h + 1) * HALF, :] = value.T.astype(BF16)
    for copy in started + fourth:
        copy.wait_send()


def grid_kernel(
    field, b_tab, bias, gt, kron, out, f_v, b_v, bias_v, o_v, field_sem, basis_sem, out_sem
):
    me_z = lax.axis_index("gz")
    chans, planes, rows, depth = f_v.shape
    loads = []
    for x in range(planes):
        one = pltpu.make_async_copy(field.at[:, x], f_v.at[:, x], field_sem.at[x])
        two = pltpu.make_async_copy(b_tab.at[me_z, x], b_v.at[x], basis_sem.at[x])
        one.start()
        two.start()
        loads.append((one, two))
    for o in range(chans):
        bias_v[o * rows:(o + 1) * rows, :] = jnp.full((rows, depth), bias[o], F32)
    stores = []
    scale = math.sqrt(2.0 / math.pi)
    for x in range(planes):
        for load in loads[x]:
            load.wait()
        grid = f_v[:, x].reshape(chans * rows, depth)
        value = jnp.dot(kron[...], grid, preferred_element_type=F32)
        value += jnp.dot(gt[...], b_v[x], preferred_element_type=F32)
        value += bias_v[...]
        inner = value * (scale + (scale * 0.044715) * (value * value))
        small = 0.5 * value
        value = small + small * jnp.tanh(inner)
        o_v[:, x] = value.astype(BF16).reshape(chans, rows, depth)
        store = pltpu.make_async_copy(o_v.at[:, x], out.at[:, x], out_sem.at[x])
        store.start()
        stores.append(store)
    for store in stores:
        store.wait()


def shards(n_y, n_z, field, spectral_weight, point_weight, bias):
    chans, planes, rows, depth = field.shape
    first_share, depth_share = spectral_weight.shape[:2]
    assert depth_share == SHARE and chans * rows == 2 * HALF and first_share <= KY
    assert n_y % planes == 0 and depth_share * n_z == KZ
    a_tab, b_tab, ay_tab, sy_tab = tables(n_y, n_z, planes, rows, depth, first_share)
    group = n_y // planes
    vmem = pl.BlockSpec(memory_space=pltpu.VMEM)
    any_ = pl.BlockSpec(memory_space=pl.ANY)
    wide = 2 * HALF
    dma = pltpu.SemaphoreType.DMA
    gt, kron = pl.pallas_call(
        functools.partial(spectral_kernel, n_y, n_z),
        out_shape=(
            jax.ShapeDtypeStruct((wide, planes * KZ), BF16),
            jax.ShapeDtypeStruct((wide, wide), BF16),
        ),
        in_specs=[any_, any_, any_, vmem, any_, any_],
        out_specs=(vmem, vmem),
        scratch_shapes=[
            pltpu.VMEM(field.shape, BF16),
            pltpu.VMEM(a_tab.shape[1:], BF16),
            pltpu.VMEM(spectral_weight.shape, BF16),
            pltpu.VMEM(ay_tab.shape[1:], F32),
            pltpu.VMEM(sy_tab.shape[1:], F32),
            pltpu.VMEM((wide, chans * chans), BF16),
            pltpu.VMEM((chans * chans, wide), BF16),
            pltpu.VMEM((n_z * planes, 16, HALF), BF16),
            pltpu.VMEM((n_z - 1, planes, 16, HALF), BF16),
            pltpu.VMEM((planes, 16, HALF), BF16),
            pltpu.VMEM((n_y, 16, HALF), BF16),
            pltpu.VMEM((first_share, SHARE, wide), F32),
            pltpu.VMEM((first_share, SHARE, wide), F32),
            pltpu.VMEM((n_y, 16, HALF), BF16),
            pltpu.VMEM((n_y, 16, HALF), BF16),
            pltpu.VMEM((n_z * planes, 16, HALF), BF16),
            dma((6,)),
            dma((n_z - 1, planes)),
            dma((n_z - 1, planes)),
            dma((n_y,)),
            dma((n_y,)),
            dma((n_y,)),
            dma((n_y,)),
            dma((n_z - 1, planes)),
            dma((n_z - 1, planes)),
        ],
        compiler_params=pltpu.CompilerParams(
            collective_id=0, has_side_effects=True, vmem_limit_bytes=40 * 1024 * 1024
        ),
        name="spectral",
    )(field, a_tab, spectral_weight, point_weight, ay_tab, sy_tab)
    return pl.pallas_call(
        grid_kernel,
        out_shape=jax.ShapeDtypeStruct(field.shape, BF16),
        in_specs=[any_, any_, pl.BlockSpec(memory_space=pltpu.SMEM), vmem, vmem],
        out_specs=any_,
        scratch_shapes=[
            pltpu.VMEM(field.shape, BF16),
            pltpu.VMEM(b_tab.shape[1:], BF16),
            pltpu.VMEM((chans * rows, depth), F32),
            pltpu.VMEM(field.shape, BF16),
            dma((planes,)),
            dma((planes,)),
            dma((planes,)),
        ],
        compiler_params=pltpu.CompilerParams(vmem_limit_bytes=40 * 1024 * 1024),
        name="grid",
    )(field, b_tab, bias, gt, kron)


def solution(mesh):
    return jax.shard_map(
        functools.partial(shards, mesh.shape["gy"], mesh.shape["gz"]),
        mesh=mesh,
        in_specs=(P(None, None, "gy", "gz"), P("gy", "gz", None), P(), P()),
        out_specs=P(None, None, "gy", "gz"),
        check_vma=False,
    )
```

time: 202 us -> 39.6 us (0.20)
  waiting for transfers between devices: 81 us -> 0 us
  blocking collectives: 50.2 us -> 0 us
  matrix products: 31.9 us -> 0 us
  Pallas kernels: 0 us -> 31.5 us
  between operations: 13.6 us -> 0.03 us
  local copies, waits for them, and re-layouts: 20.9 us -> 7.42 us
  other arithmetic: 2.69 us -> 0 us
    unnamed x3 -> x0, waiting for transfers between devices: 61.6 us -> none
    all_gather x2 -> x0, blocking collectives: 50.2 us -> none  [the longest x1 43.9 us: shards(): full_modes = lax.all_gather(widened, 'gy', axis=1, tiled=True)]
    dot_general x7 -> x0, matrix products: 31.9 us -> none  [the longest x1 7.46 us: shards(): spatial = jnp.einsum('cxyk,kz->cxyz', spatial, synth_z, precision=highest)]
    pallas_call x0 -> x2, Pallas kernels: none -> 31.5 us  [the longest x1 23.7 us: shards(): pl.pallas_call(functools.partial(spectral_kernel, n_y, n_z), out_shape=(j...]
    reduce_scatter x1 -> x0, waiting for transfers between devices: 19.4 us -> none  [shards(): owned = lax.psum_scatter(reduced, 'gz', scatter_dimension=2, tiled=True)]
    unnamed x15 -> x16, local copies, waits for them, and re-layouts: 14 us -> 7.42 us
    dot_general x2 -> x0, local copies, waits for them, and re-layouts: 3.83 us -> none  [the longest x1 3.71 us: shards(): jnp.einsum('cxyz,kz->cxyk', field, analysis_z, preferred_element_type=jnp...]
    unnamed x1 -> x0, other arithmetic: 2.64 us -> none
  transfers between devices with their start and end apart: 2 -> 0, of which waited for: 2 -> 0; matrix products, arithmetic and copies ran while one was open for 3% -> 0% of each run, Pallas kernels for 0% -> 0%
where the time goes in v1:
time: 39.6 us; the launch traced here: 39 us
  Pallas kernels  31.5 us (80%)
  local copies, waits for them, and re-layouts  7.42 us (19%)
    pallas_call x1, Pallas kernels, shards(): pl.pallas_call(functools.partial(spectral_kernel, n_y, n_z), out_shape=(j...  23.7 us
    pallas_call x1, Pallas kernels, shards(): pl.pallas_call(grid_kernel, out_shape=jax.ShapeDtypeStruct(field.shape, B...  7.78 us
    unnamed x16, local copies, waits for them, and re-layouts  7.42 us

profile of v1, /device:TPU:1, one launch (start us, length us, event | category | flops | bytes accessed | tf_op | source)
XLA Modules:
  0.0 39.0 jit_solution(11407608711911374741)
XLA Ops:
  0.0 0.0 copy-start
  0.0 1.6 %copy-done = bf16[32,8,16,256]{3,2,1,0:T(8,128)(2,1)S(1)} copy-done((bf16[32,8,16,256]{3,2,1,0:T(8,128)(2,1)S(1)}, bf16[32,8,16,256]{3,2,1,0:T(8,128)(2,1)}, u32[]{:S(2)}) %copy-start) | copy-done | bytes 2097176
  1.6 0.0 copy-start.2
  1.6 2.2 %copy-done.2 = bf16[4,8,256,256]{3,2,1,0:T(8,128)(2,1)S(1)} copy-done((bf16[4,8,256,256]{3,2,1,0:T(8,128)(2,1)S(1)}, bf16[4,8,256,256]{3,2,1,0:T(8,128)(2,1)}, u32[]{:S(2)}) %copy-start.2) | copy-done | bytes 4194328
  3.8 0.0 copy-start.3
  3.8 1.0 %copy-done.3 = bf16[32,8,1024]{2,1,0:T(8,128)(2,1)S(1)} copy-done((bf16[32,8,1024]{2,1,0:T(8,128)(2,1)S(1)}, bf16[32,8,1024]{2,1,0:T(8,128)(2,1)}, u32[]{:S(2)}) %copy-start.3) | copy-done | bytes 524312
  4.8 0.0 copy-start.4
  4.8 0.9 %copy-done.4 = f32[1,8,32,256]{3,2,1,0:T(8,128)S(1)} copy-done((f32[1,8,32,256]{3,2,1,0:T(8,128)S(1)}, f32[1,8,32,256]{3,2,1,0:T(8,128)}, u32[]{:S(2)}) %copy-start.4) | copy-done | bytes 262168
  5.8 0.0 copy-start.5
  5.8 0.9 %copy-done.5 = f32[1,32,8,256]{3,2,1,0:T(8,128)S(1)} copy-done((f32[1,32,8,256]{3,2,1,0:T(8,128)S(1)}, f32[1,32,8,256]{3,2,1,0:T(8,128)}, u32[]{:S(2)}) %copy-start.5) | copy-done | bytes 262168
  6.7 0.0 copy-start.6
  6.7 0.7 %copy-done.6 = bf16[32,32]{1,0:T(8,128)(2,1)S(1)} copy-done((bf16[32,32]{1,0:T(8,128)(2,1)S(1)}, bf16[32,32]{1,0:T(8,128)(2,1)}, u32[]{:S(2)}) %copy-start.6) | copy-done | bytes 2072
  7.4 0.0 copy-start.1
  7.4 0.0 copy-start.7
  7.4 23.7 %spectral.1 = (bf16[512,256]{1,0:T(8,128)(2,1)S(1)}, bf16[512,512]{1,0:T(8,128)(2,1)S(1)}) custom-call(bf16[32,8,16,256]{3,2,1,0:T(8,128)(2,1)S(1)} %copy-done, bf16[4,8,256,256]{3,2,1,0:T(8,128)(2,1)S(1)} %copy-done.2, bf16[32,8,1024]{2,1,0:T(8,128)(2,1)S(1)} %copy-done.3, bf16[32,32]{1,0:T(8,128)(2,1)S(1)} %copy-done.6, f32[1,32,8,256]{3,2,1,0:T(8,128)S(1)} %copy-done.5, ...), custom_call_target="tpu_custom_call" | custom-call | tf_op jit(solution)/shard_map/spectral/pallas_call | solution.py:302
  31.2 0.0 copy-done.1
  31.2 0.0 copy-done.7
  31.2 7.8 %grid.1 = bf16[32,8,16,256]{3,2,1,0:T(8,128)(2,1)} custom-call(bf16[32,8,16,256]{3,2,1,0:T(8,128)(2,1)S(1)} %copy-done, bf16[4,8,256,256]{3,2,1,0:T(8,128)(2,1)S(1)} %copy-done.1, f32[32]{0:T(128)S(1)} %copy-done.7, bf16[512,256]{1,0:T(8,128)(2,1)S(1)} %get-tuple-element.7.gt, bf16[512,512]{1,0:T(8,128)(2,1)S(1)} %get-tuple-element.8.kron), custom_call_target="tpu_custom_call" | custom-call | tf_op jit(solution)/shard_map/grid/pallas_call | solution.py:342
Async XLA Ops:
  0.0 1.6 %copy-start = (bf16[32,8,16,256]{3,2,1,0:T(8,128)(2,1)S(1)}, bf16[32,8,16,256]{3,2,1,0:T(8,128)(2,1)}, u32[]{:S(2)}) copy-start(bf16[32,8,16,256]{3,2,1,0:T(8,128)(2,1)} %field.3) | copy-start | bytes 6291460
  1.6 2.2 %copy-start.2 = (bf16[4,8,256,256]{3,2,1,0:T(8,128)(2,1)S(1)}, bf16[4,8,256,256]{3,2,1,0:T(8,128)(2,1)}, u32[]{:S(2)}) copy-start(bf16[4,8,256,256]{3,2,1,0:T(8,128)(2,1)} %constant.8.clone.a_tab) | copy-start | bytes 12582916
  3.8 1.0 %copy-start.3 = (bf16[32,8,1024]{2,1,0:T(8,128)(2,1)S(1)}, bf16[32,8,1024]{2,1,0:T(8,128)(2,1)}, u32[]{:S(2)}) copy-start(bf16[32,8,1024]{2,1,0:T(8,128)(2,1)} %weight.1) | copy-start | bytes 1572868
  4.8 0.9 %copy-start.4 = (f32[1,8,32,256]{3,2,1,0:T(8,128)S(1)}, f32[1,8,32,256]{3,2,1,0:T(8,128)}, u32[]{:S(2)}) copy-start(f32[1,8,32,256]{3,2,1,0:T(8,128)} %constant.10.clone.sy_tab) | copy-start | bytes 786436
  5.8 0.9 %copy-start.5 = (f32[1,32,8,256]{3,2,1,0:T(8,128)S(1)}, f32[1,32,8,256]{3,2,1,0:T(8,128)}, u32[]{:S(2)}) copy-start(f32[1,32,8,256]{3,2,1,0:T(8,128)} %constant.9.clone.ay_tab) | copy-start | bytes 786436
  6.7 0.7 %copy-start.6 = (bf16[32,32]{1,0:T(8,128)(2,1)S(1)}, bf16[32,32]{1,0:T(8,128)(2,1)}, u32[]{:S(2)}) copy-start(bf16[32,32]{1,0:T(8,128)(2,1)} %point.1) | copy-start | bytes 6148
  7.4 23.7 %copy-start.1 = (bf16[4,8,256,256]{3,2,1,0:T(8,128)(2,1)S(1)}, bf16[4,8,256,256]{3,2,1,0:T(8,128)(2,1)}, u32[]{:S(2)}) copy-start(bf16[4,8,256,256]{3,2,1,0:T(8,128)(2,1)} %constant.11.clone.b_tab) | copy-start | bytes 12582916
  7.4 23.7 %copy-start.7 = (f32[32]{0:T(128)S(1)}, f32[32]{0:T(128)}, u32[]{:S(2)}) copy-start(f32[32]{0:T(128)} %bias.1) | copy-start | bytes 388

commit v2 on v1

v2 whole, which is shorter than its diff:
```python
import functools
import math

import jax
import jax.numpy as jnp
import ml_dtypes
import numpy as np
from jax import lax
from jax.experimental import pallas as pl
from jax.experimental.pallas import tpu as pltpu
from jax.sharding import PartitionSpec as P

KY = 32
KZ = 32
BF16 = jnp.bfloat16
F32 = jnp.float32
MESH = pl.DeviceIdType.MESH
SHARE = 8
HALF = 256


def basis(count, length, norm):
    modes = np.arange(count)[:, None]
    spots = np.arange(length)[None, :]
    value = norm * np.cos(np.pi * modes * (spots + 0.5) / length)
    return np.where(modes == 0, value * math.sqrt(0.5), value)


def tables(n_y, n_z, planes, rows, depth, first_share):
    total_rows, total_depth = rows * n_y, depth * n_z
    az = basis(KZ, total_depth, math.sqrt(2.0 / total_depth))
    az = az.astype(np.float32).astype(ml_dtypes.bfloat16).astype(np.float64)
    ax = basis(planes, planes, math.sqrt(2.0 / planes))
    sz = basis(KZ, total_depth, math.sqrt(2.0 / KZ))

    def joint(x_basis, z_basis):
        z = z_basis.reshape(n_z, SHARE, n_z, depth)
        both = np.einsum("ix,bkdz->dxbikz", x_basis, z)
        return both.reshape(n_z, planes, planes * KZ, depth).astype(ml_dtypes.bfloat16)

    ay = basis(KY, total_rows, math.sqrt(2.0 / total_rows))
    sy = basis(KY, total_rows, math.sqrt(2.0 / KY))
    blocks = KY // first_share

    def lanes(y_basis):
        parts = y_basis.reshape(blocks, first_share, n_y, rows)
        return np.tile(parts, (1, 1, 1, HALF // rows)).astype(np.float32)

    analysis_y = lanes(ay)
    synth_y = np.ascontiguousarray(np.swapaxes(lanes(sy), 1, 2))
    return joint(ax, az), joint(ax, sz), analysis_y, synth_y


def bits(count):
    assert count & (count - 1) == 0
    return count.bit_length() - 1


def select(shape, row_of, column_of):
    r = row_of(lax.broadcasted_iota(jnp.int32, shape, 0))
    c = column_of(lax.broadcasted_iota(jnp.int32, shape, 1))
    return jnp.where(r == c, 1.0, 0.0).astype(F32)


def spectral_kernel(
    n_y, n_z, field, a_tab, b_tab, weight, point, bias, ay_tab, sy_tab, local, gt_out, b_out,
    f_v, a_v, w_v, p_v, bias_s, bias_v, ay_v, sy_v, e1, e2, spread, kron,
    part, got1, owned, got2, u_v, m_v, tout, got3, modes,
    load_sem, grid_sem, a_sem, send1, recv1, send2, recv2, send3, recv3, send4, recv4,
):
    me_y, me_z = lax.axis_index("gy"), lax.axis_index("gz")
    chans, planes, rows, depth = f_v.shape
    pairs = planes // 2
    group = n_y // planes
    first_share = w_v.shape[0]
    mine, place = lax.div(me_y, group), lax.rem(me_y, group)
    block = place if first_share < KY else 0
    others = [(d, t) for d in range(planes) for t in range(group)][1:]

    def flip(index, mask):
        for k in range(bits(planes)):
            if mask >> k & 1:
                bit = lax.rem(lax.div(index, 1 << k), 2)
                index = index + (1 << k) * (1 - 2 * bit)
        return index

    def at(d, t):
        return flip(mine, d) * group + lax.rem(place + t, group)

    def came(d, t):
        return flip(mine, d) * group + lax.rem(place - t + group, group)

    def peer(e):
        return lax.rem(me_z + e, n_z)

    barrier = pltpu.get_barrier_semaphore()
    for e in range(1, n_z):
        pl.semaphore_signal(
            barrier, inc=1, device_id=(me_y, peer(e)), device_id_type=MESH
        )
    for d, t in others:
        pl.semaphore_signal(
            barrier, inc=1, device_id=(at(d, t), me_z), device_id_type=MESH
        )

    half = chans // 2
    grids = []
    for x in range(planes):
        one = pltpu.make_async_copy(a_tab.at[me_z, x], a_v.at[x], a_sem.at[x])
        two = pltpu.make_async_copy(
            field.at[0:half, x], f_v.at[0:half, x], grid_sem.at[x]
        )
        one.start()
        two.start()
        grids.append((one, two))
    loads = [
        pltpu.make_async_copy(field.at[half:chans], f_v.at[half:chans], load_sem.at[0]),
        pltpu.make_async_copy(point, p_v, load_sem.at[1]),
        pltpu.make_async_copy(bias, bias_s, load_sem.at[2]),
        pltpu.make_async_copy(weight, w_v, load_sem.at[3]),
        pltpu.make_async_copy(ay_tab.at[block], ay_v, load_sem.at[4]),
        pltpu.make_async_copy(sy_tab.at[block], sy_v, load_sem.at[5]),
        pltpu.make_async_copy(b_tab.at[me_z], b_out, load_sem.at[6]),
    ]
    for load in loads:
        load.start()

    e1[...] = select(
        e1.shape, lambda r: r >> bits(rows), lambda c: c >> bits(chans)
    ).astype(BF16)
    e2[...] = select(
        e2.shape, lambda r: r & (chans - 1), lambda c: c >> bits(rows)
    ).astype(BF16)
    spread[...] = select(spread.shape, lambda r: r >> bits(rows), lambda c: c).astype(BF16)

    pair_order = range(pairs - 1, -1, -1)
    started = []
    first = {}
    for h in range(2):
        if h == 1:
            loads[0].wait()
        total = jnp.zeros((planes * KZ, HALF), F32)
        for x in range(planes):
            if h == 0:
                for load in grids[x]:
                    load.wait()
            grid = f_v[h * half:(h + 1) * half, x].reshape(HALF, depth)
            total += lax.dot_general(
                a_v[x], grid, (((1,), (1,)), ((), ())), preferred_element_type=F32
            )
        part[h] = total.reshape(n_z * pairs, 2 * SHARE, HALF).astype(BF16)
        if h == 0:
            pl.semaphore_wait(barrier, n_z - 1 + len(others))
        for p in pair_order:
            ip = lax.div(flip(mine, 2 * p), 2)
            for e in range(1, n_z):
                copy = pltpu.make_async_remote_copy(
                    src_ref=part.at[h, peer(e) * pairs + ip],
                    dst_ref=got1.at[e - 1, h, ip],
                    send_sem=send1.at[e - 1, h, p],
                    recv_sem=recv1.at[e - 1, h, p],
                    device_id=(me_y, peer(e)),
                    device_id_type=MESH,
                )
                copy.start()
                first[e, h, p] = copy
                started.append(copy)

    loads[1].wait()
    wide = lax.dot_general(
        spread[...], p_v[...], (((1,), (1,)), ((), ())), preferred_element_type=F32
    ).astype(BF16)
    wide = lax.dot_general(
        wide, spread[...], (((1,), (1,)), ((), ())), preferred_element_type=F32
    )
    same = select(wide.shape, lambda r: r & (rows - 1), lambda c: c & (rows - 1))
    kron[...] = (wide * same).astype(BF16)
    loads[2].wait()
    for o in range(chans):
        bias_v[o * rows:(o + 1) * rows, :] = jnp.full((rows, depth), bias_s[o], F32)

    def pointwise(x):
        grid = f_v[:, x].reshape(chans * rows, depth)
        value = jnp.dot(kron[...], grid, preferred_element_type=F32)
        local[x] = value + bias_v[...]

    pointwise(0)

    second = {}
    for p in pair_order:
        ip = lax.div(flip(mine, 2 * p), 2)
        sums = []
        for h in range(2):
            total = part[h, me_z * pairs + ip].astype(F32)
            for e in range(1, n_z):
                first[e, h, p].wait_recv()
                total += got1[e - 1, h, ip].astype(F32)
            sums.append(total)
        for odd in range(2):
            side = slice(odd * SHARE, (odd + 1) * SHARE)
            owned[ip * 2 + odd] = jnp.concatenate(
                [sums[0][side], sums[1][side]], axis=0
            ).astype(BF16)
        for d in (2 * p + 1, 2 * p):
            for t in range(group):
                if d == 0 and t == 0:
                    continue
                copy = pltpu.make_async_remote_copy(
                    src_ref=owned.at[flip(mine, d)],
                    dst_ref=got2.at[me_y],
                    send_sem=send2.at[d * group + t],
                    recv_sem=recv2.at[d * group + t],
                    device_id=(at(d, t), me_z),
                    device_id_type=MESH,
                )
                copy.start()
                second[d, t] = copy
                started.append(copy)
    got2[me_y] = owned[mine]

    for x in range(1, 4):
        pointwise(x)

    for load in loads[3:6]:
        load.wait()
    for d, t in others:
        second[d, t].wait_recv()
    for h in range(2):
        pieces = [got2[s].astype(F32)[h * SHARE:(h + 1) * SHARE] for s in range(n_y)]
        for j in range(first_share):
            total = pieces[0] * ay_v[j, 0:1, :]
            for s in range(1, n_y):
                total += pieces[s] * ay_v[j, s:s + 1, :]
            u_v[j, :, h * HALF:(h + 1) * HALF] = total

    mode_rows = first_share * SHARE
    spectrum = jnp.dot(
        u_v[...].reshape(mode_rows, 2 * HALF).astype(BF16), e1[...], preferred_element_type=F32
    )
    terms = spectrum * w_v[...].astype(F32).reshape(mode_rows, chans * chans)
    mixed = jnp.dot(terms.astype(BF16), e2[...], preferred_element_type=F32)
    m_v[...] = mixed.reshape(first_share, SHARE, 2 * HALF)

    third = {}
    for d, t in others[::-1] + [(0, 0)]:
        target = at(d, t)
        synth = sy_v[target]
        sides = []
        for h in range(2):
            total = m_v[0, :, h * HALF:(h + 1) * HALF] * synth[0:1, :]
            for j in range(1, first_share):
                total += m_v[j, :, h * HALF:(h + 1) * HALF] * synth[j:j + 1, :]
            sides.append(total)
        value = jnp.concatenate(sides, axis=0).astype(BF16)
        if d == 0 and t == 0:
            got3[me_y] = value
            continue
        tout[target] = value
        copy = pltpu.make_async_remote_copy(
            src_ref=tout.at[target],
            dst_ref=got3.at[me_y],
            send_sem=send3.at[d * group + t],
            recv_sem=recv3.at[d * group + t],
            device_id=(target, me_z),
            device_id_type=MESH,
        )
        copy.start()
        third[d, t] = copy
        started.append(copy)

    fourth = []
    for d in [0, *range(planes - 1, 0, -1)]:
        total = None
        for t in range(group):
            if (d, t) != (0, 0):
                third[d, t].wait_recv()
            piece = got3[came(d, t)]
            if group > 1:
                piece = piece.astype(F32)
            total = piece if total is None else total + piece
        slot = me_z * planes + flip(mine, d)
        modes[slot] = total.astype(BF16)
        for e in range(1, n_z):
            copy = pltpu.make_async_remote_copy(
                src_ref=modes.at[slot],
                dst_ref=modes.at[slot],
                send_sem=send4.at[e - 1, d],
                recv_sem=recv4.at[e - 1, d],
                device_id=(me_y, peer(e)),
                device_id_type=MESH,
            )
            copy.start()
            fourth.append(copy)

    for x in range(4, planes):
        pointwise(x)
    loads[6].wait()

    for copy in fourth:
        copy.wait_recv()
    for h in range(2):
        value = modes[...].astype(F32)[:, h * SHARE:(h + 1) * SHARE, :]
        value = value.reshape(planes * KZ, HALF)
        gt_out[h * HALF:(h + 1) * HALF, :] = value.T.astype(BF16)
    for copy in started + fourth:
        copy.wait_send()


def grid_kernel(local, gt, synth, out, o_v, out_sem):
    planes, _, depth = local.shape
    chans, _, rows, _ = o_v.shape
    stores = []
    scale = math.sqrt(2.0 / math.pi)
    for x in range(planes):
        value = local[x] + jnp.dot(gt[...], synth[x], preferred_element_type=F32)
        inner = value * (scale + (scale * 0.044715) * (value * value))
        small = 0.5 * value
        value = small + small * jnp.tanh(inner)
        o_v[:, x] = value.astype(BF16).reshape(chans, rows, depth)
        store = pltpu.make_async_copy(o_v.at[:, x], out.at[:, x], out_sem.at[x])
        store.start()
        stores.append(store)
    for store in stores:
        store.wait()


def shards(n_y, n_z, field, spectral_weight, point_weight, bias):
    chans, planes, rows, depth = field.shape
    first_share, depth_share = spectral_weight.shape[:2]
    assert depth_share == SHARE and chans * rows == 2 * HALF and first_share <= KY
    assert n_y % planes == 0 and depth_share * n_z == KZ and planes % 2 == 0
    a_tab, b_tab, ay_tab, sy_tab = tables(n_y, n_z, planes, rows, depth, first_share)
    pairs = planes // 2
    vmem = pl.BlockSpec(memory_space=pltpu.VMEM)
    hbm = pl.BlockSpec(memory_space=pltpu.HBM)
    wide = 2 * HALF
    dma = pltpu.SemaphoreType.DMA
    operands = [field, a_tab, b_tab, spectral_weight, point_weight, bias, ay_tab, sy_tab]
    local, gt, synth = pl.pallas_call(
        functools.partial(spectral_kernel, n_y, n_z),
        out_shape=(
            pltpu.VMEM((planes, wide, depth), F32),
            pltpu.VMEM((wide, planes * KZ), BF16),
            pltpu.VMEM(b_tab.shape[1:], BF16),
        ),
        in_specs=[hbm] * len(operands),
        out_specs=(vmem, vmem, vmem),
        scratch_shapes=[
            pltpu.VMEM(field.shape, BF16),
            pltpu.VMEM(a_tab.shape[1:], BF16),
            pltpu.VMEM(spectral_weight.shape, BF16),
            pltpu.VMEM(point_weight.shape, BF16),
            pltpu.SMEM(bias.shape, F32),
            pltpu.VMEM((wide, depth), F32),
            pltpu.VMEM(ay_tab.shape[1:], F32),
            pltpu.VMEM(sy_tab.shape[1:], F32),
            pltpu.VMEM((wide, chans * chans), BF16),
            pltpu.VMEM((chans * chans, wide), BF16),
            pltpu.VMEM((wide, chans), BF16),
            pltpu.VMEM((wide, wide), BF16),
            pltpu.VMEM((2, n_z * pairs, 2 * SHARE, HALF), BF16),
            pltpu.VMEM((n_z - 1, 2, pairs, 2 * SHARE, HALF), BF16),
            pltpu.VMEM((planes, 2 * SHARE, HALF), BF16),
            pltpu.VMEM((n_y, 2 * SHARE, HALF), BF16),
            pltpu.VMEM((first_share, SHARE, wide), F32),
            pltpu.VMEM((first_share, SHARE, wide), F32),
            pltpu.VMEM((n_y, 2 * SHARE, HALF), BF16),
            pltpu.VMEM((n_y, 2 * SHARE, HALF), BF16),
            pltpu.VMEM((n_z * planes, 2 * SHARE, HALF), BF16),
            dma((7,)),
            dma((planes,)),
            dma((planes,)),
            dma((n_z - 1, 2, pairs)),
            dma((n_z - 1, 2, pairs)),
            dma((n_y,)),
            dma((n_y,)),
            dma((n_y,)),
            dma((n_y,)),
            dma((n_z - 1, planes)),
            dma((n_z - 1, planes)),
        ],
        compiler_params=pltpu.CompilerParams(
            collective_id=0, has_side_effects=True, vmem_limit_bytes=40 * 1024 * 1024
        ),
        name="spectral",
    )(*(pltpu.with_memory_space_constraint(value, pltpu.HBM) for value in operands))
    return pl.pallas_call(
        grid_kernel,
        out_shape=jax.ShapeDtypeStruct(field.shape, BF16),
        in_specs=[vmem] * 3,
        out_specs=hbm,
        scratch_shapes=[pltpu.VMEM(field.shape, BF16), dma((planes,))],
        compiler_params=pltpu.CompilerParams(vmem_limit_bytes=40 * 1024 * 1024),
        name="grid",
    )(local, gt, synth)


def solution(mesh):
    return jax.shard_map(
        functools.partial(shards, mesh.shape["gy"], mesh.shape["gz"]),
        mesh=mesh,
        in_specs=(P(None, None, "gy", "gz"), P("gy", "gz", None), P(), P()),
        out_specs=P(None, None, "gy", "gz"),
        check_vma=False,
    )
```

time: 39.6 us -> 26.4 us (0.67)
  local copies, waits for them, and re-layouts: 7.42 us -> 0 us
  Pallas kernels: 31.5 us -> 25.9 us
    unnamed x16 -> x0, local copies, waits for them, and re-layouts: 7.42 us -> none
    pallas_call x1, Pallas kernels: 7.78 us -> 2.46 us  [shards(): pl.pallas_call(grid_kernel, out_shape=jax.ShapeDtypeStruct(field.shape, B...]
where the time goes in v2:
time: 26.4 us; the launch traced here: 25.9 us
  Pallas kernels  25.9 us (98%)
    pallas_call x1, Pallas kernels, shards(): pl.pallas_call(functools.partial(spectral_kernel, n_y, n_z), out_shape=(p...  23.5 us
    pallas_call x1, Pallas kernels, shards(): pl.pallas_call(grid_kernel, out_shape=jax.ShapeDtypeStruct(field.shape, B...  2.46 us

profile of v2, /device:TPU:1, one launch (start us, length us, event | category | flops | bytes accessed | tf_op | source)
XLA Modules:
  0.0 25.9 jit_solution(8401986250482024967)
XLA Ops:
  0.0 23.5 %spectral.1 = (f32[8,512,256]{2,1,0:T(8,128)S(1)}, bf16[512,256]{1,0:T(8,128)(2,1)S(1)}, bf16[8,256,256]{2,1,0:T(8,128)(2,1)S(1)}) custom-call(bf16[32,8,16,256]{3,2,1,0:T(8,128)(2,1)} %field.1, bf16[4,8,256,256]{3,2,1,0:T(8,128)(2,1)} %constant.8.clone.a_tab, bf16[4,8,256,256]{3,2,1,0:T(8,128)(2,1)} %constant.9.clone.b_tab, bf16[32,8,1024]{2,1,0:T(8,128)(2,1)} %weight.1, ...), custom_call_target="tpu_custom_call" | custom-call | tf_op jit(solution)/shard_map/spectral/pallas_call | solution.py:339
  23.5 2.5 %grid.1 = bf16[32,8,16,256]{3,2,1,0:T(8,128)(2,1)} custom-call(f32[8,512,256]{2,1,0:T(8,128)S(1)} %get-tuple-element.8.local, bf16[512,256]{1,0:T(8,128)(2,1)S(1)} %get-tuple-element.9.gt, bf16[8,256,256]{2,1,0:T(8,128)(2,1)S(1)} %get-tuple-element.10.synth), custom_call_target="tpu_custom_call" | custom-call | tf_op jit(solution)/shard_map/grid/pallas_call | solution.py:387

commit v3 on v2

--- a/solution.py
+++ b/solution.py
@@ -34,8 +34,8 @@
     sz = basis(KZ, total_depth, math.sqrt(2.0 / KZ))
 
     def joint(x_basis, z_basis):
-        z = z_basis.reshape(n_z, SHARE, n_z, depth)
-        both = np.einsum("ix,bkdz->dxbikz", x_basis, z)
+        z = z_basis.reshape(n_z // 2, 2, SHARE, n_z, depth)
+        both = np.einsum("ix,hlkdz->dxlhikz", x_basis, z)
         return both.reshape(n_z, planes, planes * KZ, depth).astype(ml_dtypes.bfloat16)
 
     ay = basis(KY, total_rows, math.sqrt(2.0 / total_rows))
@@ -72,10 +72,15 @@
     chans, planes, rows, depth = f_v.shape
     pairs = planes // 2
     group = n_y // planes
+    highs = n_z // 2
+    high, low = lax.div(me_z, 2), lax.rem(me_z, 2)
+    near = high * 2 + 1 - low
     first_share = w_v.shape[0]
     mine, place = lax.div(me_y, group), lax.rem(me_y, group)
     block = place if first_share < KY else 0
-    others = [(d, t) for d in range(planes) for t in range(group)][1:]
+    others = [
+        (d, t, u) for d in range(planes) for t in range(group) for u in range(highs)
+    ][1:]
 
     def flip(index, mask):
         for k in range(bits(planes)):
@@ -90,17 +95,17 @@
     def came(d, t):
         return flip(mine, d) * group + lax.rem(place - t + group, group)
 
-    def peer(e):
-        return lax.rem(me_z + e, n_z)
+    def high_at(u):
+        return lax.rem(high + u, highs)
+
+    def arrived(blocks, semaphore):
+        pltpu.make_async_copy(blocks, blocks, semaphore).wait()
 
     barrier = pltpu.get_barrier_semaphore()
-    for e in range(1, n_z):
+    pl.semaphore_signal(barrier, inc=1, device_id=(me_y, near), device_id_type=MESH)
+    for d, t, u in others:
         pl.semaphore_signal(
-            barrier, inc=1, device_id=(me_y, peer(e)), device_id_type=MESH
-        )
-    for d, t in others:
-        pl.semaphore_signal(
-            barrier, inc=1, device_id=(at(d, t), me_z), device_id_type=MESH
+            barrier, inc=1, device_id=(at(d, t), high_at(u) * 2 + low), device_id_type=MESH
         )
 
     half = chans // 2
@@ -128,14 +133,8 @@
     e1[...] = select(
         e1.shape, lambda r: r >> bits(rows), lambda c: c >> bits(chans)
     ).astype(BF16)
-    e2[...] = select(
-        e2.shape, lambda r: r & (chans - 1), lambda c: c >> bits(rows)
-    ).astype(BF16)
-    spread[...] = select(spread.shape, lambda r: r >> bits(rows), lambda c: c).astype(BF16)
 
     pair_order = range(pairs - 1, -1, -1)
-    started = []
-    first = {}
     for h in range(2):
         if h == 1:
             loads[0].wait()
@@ -148,23 +147,51 @@
             total += lax.dot_general(
                 a_v[x], grid, (((1,), (1,)), ((), ())), preferred_element_type=F32
             )
-        part[h] = total.reshape(n_z * pairs, 2 * SHARE, HALF).astype(BF16)
+        part[h] = total.reshape(2, highs * pairs, 2 * SHARE, HALF).astype(BF16)
         if h == 0:
-            pl.semaphore_wait(barrier, n_z - 1 + len(others))
-        for p in pair_order:
-            ip = lax.div(flip(mine, 2 * p), 2)
-            for e in range(1, n_z):
-                copy = pltpu.make_async_remote_copy(
-                    src_ref=part.at[h, peer(e) * pairs + ip],
-                    dst_ref=got1.at[e - 1, h, ip],
-                    send_sem=send1.at[e - 1, h, p],
-                    recv_sem=recv1.at[e - 1, h, p],
-                    device_id=(me_y, peer(e)),
-                    device_id_type=MESH,
-                )
-                copy.start()
-                first[e, h, p] = copy
-                started.append(copy)
+            pl.semaphore_wait(barrier, 1 + len(others))
+        pltpu.make_async_remote_copy(
+            src_ref=part.at[h, 1 - low],
+            dst_ref=got1.at[h],
+            send_sem=send1,
+            recv_sem=recv1.at[h],
+            device_id=(me_y, near),
+            device_id_type=MESH,
+        ).start()
+
+    e2[...] = select(
+        e2.shape, lambda r: r & (chans - 1), lambda c: c >> bits(rows)
+    ).astype(BF16)
+    for h in range(2):
+        arrived(got1.at[h], recv1.at[h])
+    for p in pair_order:
+        ip = lax.div(flip(mine, 2 * p), 2)
+        for u in range(highs):
+            slot = high_at(u) * pairs + ip
+            sums = []
+            for h in range(2):
+                sums.append(part[h, low, slot].astype(F32) + got1[h, slot].astype(F32))
+            for odd in range(2):
+                side = slice(odd * SHARE, (odd + 1) * SHARE)
+                owned[high_at(u) * planes + ip * 2 + odd] = jnp.concatenate(
+                    [sums[0][side], sums[1][side]], axis=0
+                ).astype(BF16)
+        for d in (2 * p + 1, 2 * p):
+            for t in range(group):
+                for u in range(highs):
+                    if d == 0 and t == 0 and u == 0:
+                        continue
+                    pltpu.make_async_remote_copy(
+                        src_ref=owned.at[high_at(u) * planes + flip(mine, d)],
+                        dst_ref=got2.at[high * n_y + me_y],
+                        send_sem=send2,
+                        recv_sem=recv2,
+                        device_id=(at(d, t), high_at(u) * 2 + low),
+                        device_id_type=MESH,
+                    ).start()
+    got2[high * n_y + me_y] = owned[high * planes + mine]
+
+    spread[...] = select(spread.shape, lambda r: r >> bits(rows), lambda c: c).astype(BF16)
 
     loads[1].wait()
     wide = lax.dot_general(
@@ -184,49 +211,19 @@
         value = jnp.dot(kron[...], grid, preferred_element_type=F32)
         local[x] = value + bias_v[...]
 
-    pointwise(0)
-
-    second = {}
-    for p in pair_order:
-        ip = lax.div(flip(mine, 2 * p), 2)
-        sums = []
-        for h in range(2):
-            total = part[h, me_z * pairs + ip].astype(F32)
-            for e in range(1, n_z):
-                first[e, h, p].wait_recv()
-                total += got1[e - 1, h, ip].astype(F32)
-            sums.append(total)
-        for odd in range(2):
-            side = slice(odd * SHARE, (odd + 1) * SHARE)
-            owned[ip * 2 + odd] = jnp.concatenate(
-                [sums[0][side], sums[1][side]], axis=0
-            ).astype(BF16)
-        for d in (2 * p + 1, 2 * p):
-            for t in range(group):
-                if d == 0 and t == 0:
-                    continue
-                copy = pltpu.make_async_remote_copy(
-                    src_ref=owned.at[flip(mine, d)],
-                    dst_ref=got2.at[me_y],
-                    send_sem=send2.at[d * group + t],
-                    recv_sem=recv2.at[d * group + t],
-                    device_id=(at(d, t), me_z),
-                    device_id_type=MESH,
-                )
-                copy.start()
-                second[d, t] = copy
-                started.append(copy)
-    got2[me_y] = owned[mine]
-
-    for x in range(1, 4):
+    for x in range(4):
         pointwise(x)
 
     for load in loads[3:6]:
         load.wait()
-    for d, t in others:
-        second[d, t].wait_recv()
+    arrived(got2.at[0:len(others)], recv2)
     for h in range(2):
-        pieces = [got2[s].astype(F32)[h * SHARE:(h + 1) * SHARE] for s in range(n_y)]
+        pieces = []
+        for s in range(n_y):
+            total = got2[s].astype(F32)
+            for u in range(1, highs):
+                total += got2[u * n_y + s].astype(F32)
+            pieces.append(total[h * SHARE:(h + 1) * SHARE])
         for j in range(first_share):
             total = pieces[0] * ay_v[j, 0:1, :]
             for s in range(1, n_y):
@@ -241,69 +238,72 @@
     mixed = jnp.dot(terms.astype(BF16), e2[...], preferred_element_type=F32)
     m_v[...] = mixed.reshape(first_share, SHARE, 2 * HALF)
 
-    third = {}
-    for d, t in others[::-1] + [(0, 0)]:
-        target = at(d, t)
-        synth = sy_v[target]
-        sides = []
-        for h in range(2):
-            total = m_v[0, :, h * HALF:(h + 1) * HALF] * synth[0:1, :]
-            for j in range(1, first_share):
-                total += m_v[j, :, h * HALF:(h + 1) * HALF] * synth[j:j + 1, :]
-            sides.append(total)
-        value = jnp.concatenate(sides, axis=0).astype(BF16)
-        if d == 0 and t == 0:
-            got3[me_y] = value
-            continue
-        tout[target] = value
-        copy = pltpu.make_async_remote_copy(
-            src_ref=tout.at[target],
-            dst_ref=got3.at[me_y],
-            send_sem=send3.at[d * group + t],
-            recv_sem=recv3.at[d * group + t],
-            device_id=(target, me_z),
-            device_id_type=MESH,
-        )
-        copy.start()
-        third[d, t] = copy
-        started.append(copy)
-
-    fourth = []
-    for d in [0, *range(planes - 1, 0, -1)]:
-        total = None
-        for t in range(group):
-            if (d, t) != (0, 0):
-                third[d, t].wait_recv()
-            piece = got3[came(d, t)]
-            if group > 1:
-                piece = piece.astype(F32)
-            total = piece if total is None else total + piece
-        slot = me_z * planes + flip(mine, d)
-        modes[slot] = total.astype(BF16)
-        for e in range(1, n_z):
-            copy = pltpu.make_async_remote_copy(
-                src_ref=modes.at[slot],
-                dst_ref=modes.at[slot],
-                send_sem=send4.at[e - 1, d],
-                recv_sem=recv4.at[e - 1, d],
-                device_id=(me_y, peer(e)),
-                device_id_type=MESH,
-            )
-            copy.start()
-            fourth.append(copy)
+    sets = [range(1 << k, 2 << k) for k in range(bits(planes) - 1, 0, -1)] + [range(2)]
+    landing = modes if group == 1 else got3
+
+    def land(index, sender):
+        start = low * highs * planes if group == 1 else 0
+        return start + index * n_y + sender
+
+    for c, members in enumerate(sets):
+        for d in members[::-1]:
+            for t in range(group - 1, -1, -1):
+                target = at(d, t)
+                sides = []
+                for h in range(2):
+                    total = m_v[0, :, h * HALF:(h + 1) * HALF] * sy_v[target, 0:1, :]
+                    for j in range(1, first_share):
+                        total += m_v[j, :, h * HALF:(h + 1) * HALF] * sy_v[target, j:j + 1, :]
+                    sides.append(total)
+                tout[target] = jnp.concatenate(sides, axis=0).astype(BF16)
+                for u in range(highs):
+                    if d == 0 and t == 0 and u == 0:
+                        landing[land(high, me_y)] = tout[target]
+                        continue
+                    pltpu.make_async_remote_copy(
+                        src_ref=tout.at[target],
+                        dst_ref=landing.at[land(high, me_y)],
+                        send_sem=send3,
+                        recv_sem=recv3.at[c],
+                        device_id=(target, high_at(u) * 2 + low),
+                        device_id_type=MESH,
+                    ).start()
 
     for x in range(4, planes):
         pointwise(x)
     loads[6].wait()
 
-    for copy in fourth:
-        copy.wait_recv()
+    for c, members in enumerate(sets):
+        count = len(members) * group * highs - (1 if 0 in members else 0)
+        arrived(landing.at[0:count], recv3.at[c])
+        size = len(members)
+        first = lax.div(flip(mine, members[0]), size) * size
+        for index in range(highs):
+            start = (low * highs + index) * planes
+            if group > 1:
+                for d in members:
+                    total = landing[land(index, came(d, 0))].astype(F32)
+                    for t in range(1, group):
+                        total += landing[land(index, came(d, t))].astype(F32)
+                    modes[start + flip(mine, d)] = total.astype(BF16)
+            pltpu.make_async_remote_copy(
+                src_ref=modes.at[pl.ds(start + first, size)],
+                dst_ref=modes.at[pl.ds(start + first, size)],
+                send_sem=send4,
+                recv_sem=recv4,
+                device_id=(me_y, near),
+                device_id_type=MESH,
+            ).start()
+
+    arrived(modes.at[0:highs * planes], recv4)
     for h in range(2):
         value = modes[...].astype(F32)[:, h * SHARE:(h + 1) * SHARE, :]
         value = value.reshape(planes * KZ, HALF)
         gt_out[h * HALF:(h + 1) * HALF, :] = value.T.astype(BF16)
-    for copy in started + fourth:
-        copy.wait_send()
+    arrived(got1, send1)
+    arrived(got2.at[0:len(others)], send2)
+    arrived(got2.at[0:len(others)], send3)
+    arrived(modes.at[0:highs * planes], send4)
 
 
 def grid_kernel(local, gt, synth, out, o_v, out_sem):
@@ -328,9 +328,9 @@
     chans, planes, rows, depth = field.shape
     first_share, depth_share = spectral_weight.shape[:2]
     assert depth_share == SHARE and chans * rows == 2 * HALF and first_share <= KY
-    assert n_y % planes == 0 and depth_share * n_z == KZ and planes % 2 == 0
+    assert n_y % planes == 0 and depth_share * n_z == KZ and planes % 2 == 0 and n_z % 2 == 0
     a_tab, b_tab, ay_tab, sy_tab = tables(n_y, n_z, planes, rows, depth, first_share)
-    pairs = planes // 2
+    pairs, highs = planes // 2, n_z // 2
     vmem = pl.BlockSpec(memory_space=pltpu.VMEM)
     hbm = pl.BlockSpec(memory_space=pltpu.HBM)
     wide = 2 * HALF
@@ -358,26 +358,26 @@
             pltpu.VMEM((chans * chans, wide), BF16),
             pltpu.VMEM((wide, chans), BF16),
             pltpu.VMEM((wide, wide), BF16),
-            pltpu.VMEM((2, n_z * pairs, 2 * SHARE, HALF), BF16),
-            pltpu.VMEM((n_z - 1, 2, pairs, 2 * SHARE, HALF), BF16),
-            pltpu.VMEM((planes, 2 * SHARE, HALF), BF16),
-            pltpu.VMEM((n_y, 2 * SHARE, HALF), BF16),
+            pltpu.VMEM((2, 2, highs * pairs, 2 * SHARE, HALF), BF16),
+            pltpu.VMEM((2, highs * pairs, 2 * SHARE, HALF), BF16),
+            pltpu.VMEM((highs * planes, 2 * SHARE, HALF), BF16),
+            pltpu.VMEM((highs * n_y, 2 * SHARE, HALF), BF16),
             pltpu.VMEM((first_share, SHARE, wide), F32),
             pltpu.VMEM((first_share, SHARE, wide), F32),
             pltpu.VMEM((n_y, 2 * SHARE, HALF), BF16),
-            pltpu.VMEM((n_y, 2 * SHARE, HALF), BF16),
+            pltpu.VMEM((highs * n_y, 2 * SHARE, HALF), BF16),
             pltpu.VMEM((n_z * planes, 2 * SHARE, HALF), BF16),
             dma((7,)),
             dma((planes,)),
             dma((planes,)),
-            dma((n_z - 1, 2, pairs)),
-            dma((n_z - 1, 2, pairs)),
-            dma((n_y,)),
-            dma((n_y,)),
-            dma((n_y,)),
-            dma((n_y,)),
-            dma((n_z - 1, planes)),
-            dma((n_z - 1, planes)),
+            dma(()),
+            dma((2,)),
+            dma(()),
+            dma(()),
+            dma(()),
+            dma((bits(planes),)),
+            dma(()),
+            dma(()),
         ],
         compiler_params=pltpu.CompilerParams(
             collective_id=0, has_side_effects=True, vmem_limit_bytes=40 * 1024 * 1024

time: 26.4 us -> 23.8 us (0.902); the launches traced: 25.9 us -> 23.6 us
  Pallas kernels: 25.9 us -> 23.6 us
    pallas_call x1, Pallas kernels: 23.5 us -> 21.2 us  [shards(): pl.pallas_call(functools.partial(spectral_kernel, n_y, n_z), out_shape=(p...]
where the time goes in v3:
time: 23.8 us; the launch traced here: 23.6 us
  Pallas kernels  23.6 us (99%)
    pallas_call x1, Pallas kernels, shards(): pl.pallas_call(functools.partial(spectral_kernel, n_y, n_z), out_shape=(p...  21.2 us
    pallas_call x1, Pallas kernels, shards(): pl.pallas_call(grid_kernel, out_shape=jax.ShapeDtypeStruct(field.shape, B...  2.46 us

profile of v3, /device:TPU:1, one launch (start us, length us, event | category | flops | bytes accessed | tf_op | source)
XLA Modules:
  0.0 23.6 jit_solution(5947329387078282263)
XLA Ops:
  0.0 21.2 %spectral.1 = (f32[8,512,256]{2,1,0:T(8,128)S(1)}, bf16[512,256]{1,0:T(8,128)(2,1)S(1)}, bf16[8,256,256]{2,1,0:T(8,128)(2,1)S(1)}) custom-call(bf16[32,8,16,256]{3,2,1,0:T(8,128)(2,1)} %field.1, bf16[4,8,256,256]{3,2,1,0:T(8,128)(2,1)} %constant.8.clone.a_tab, bf16[4,8,256,256]{3,2,1,0:T(8,128)(2,1)} %constant.9.clone.b_tab, bf16[32,8,1024]{2,1,0:T(8,128)(2,1)} %weight.1, ...), custom_call_target="tpu_custom_call" | custom-call | tf_op jit(solution)/shard_map/spectral/pallas_call | solution.py:339
  21.2 2.5 %grid.1 = bf16[32,8,16,256]{3,2,1,0:T(8,128)(2,1)} custom-call(f32[8,512,256]{2,1,0:T(8,128)S(1)} %get-tuple-element.8.local, bf16[512,256]{1,0:T(8,128)(2,1)S(1)} %get-tuple-element.9.gt, bf16[8,256,256]{2,1,0:T(8,128)(2,1)S(1)} %get-tuple-element.10.synth), custom_call_target="tpu_custom_call" | custom-call | tf_op jit(solution)/shard_map/grid/pallas_call | solution.py:387

commit v4 on v3

--- a/solution.py
+++ b/solution.py
@@ -47,8 +47,9 @@
         return np.tile(parts, (1, 1, 1, HALF // rows)).astype(np.float32)
 
     analysis_y = lanes(ay)
-    synth_y = np.ascontiguousarray(np.swapaxes(lanes(sy), 1, 2))
-    return joint(ax, az), joint(ax, sz), analysis_y, synth_y
+    synth_y = np.ascontiguousarray(np.swapaxes(lanes(0.5 * sy), 1, 2))
+    synth = joint(ax, sz).reshape(n_z, planes, 2, planes * KZ // 2, depth)
+    return joint(ax, az), synth, analysis_y, synth_y
 
 
 def bits(count):
@@ -109,6 +110,7 @@
         )
 
     half = chans // 2
+    side = planes * KZ // 2
     grids = []
     for x in range(planes):
         one = pltpu.make_async_copy(a_tab.at[me_z, x], a_v.at[x], a_sem.at[x])
@@ -125,7 +127,10 @@
         pltpu.make_async_copy(weight, w_v, load_sem.at[3]),
         pltpu.make_async_copy(ay_tab.at[block], ay_v, load_sem.at[4]),
         pltpu.make_async_copy(sy_tab.at[block], sy_v, load_sem.at[5]),
-        pltpu.make_async_copy(b_tab.at[me_z], b_out, load_sem.at[6]),
+        pltpu.make_async_copy(b_tab.at[me_z, :, low], b_out.at[:, 0:side], load_sem.at[6]),
+        pltpu.make_async_copy(
+            b_tab.at[me_z, :, 1 - low], b_out.at[:, side:2 * side], load_sem.at[7]
+        ),
     ]
     for load in loads:
         load.start()
@@ -172,9 +177,9 @@
             for h in range(2):
                 sums.append(part[h, low, slot].astype(F32) + got1[h, slot].astype(F32))
             for odd in range(2):
-                side = slice(odd * SHARE, (odd + 1) * SHARE)
+                of = slice(odd * SHARE, (odd + 1) * SHARE)
                 owned[high_at(u) * planes + ip * 2 + odd] = jnp.concatenate(
-                    [sums[0][side], sums[1][side]], axis=0
+                    [sums[0][of], sums[1][of]], axis=0
                 ).astype(BF16)
         for d in (2 * p + 1, 2 * p):
             for t in range(group):
@@ -201,10 +206,10 @@
         wide, spread[...], (((1,), (1,)), ((), ())), preferred_element_type=F32
     )
     same = select(wide.shape, lambda r: r & (rows - 1), lambda c: c & (rows - 1))
-    kron[...] = (wide * same).astype(BF16)
+    kron[...] = (wide * (0.5 * same)).astype(BF16)
     loads[2].wait()
     for o in range(chans):
-        bias_v[o * rows:(o + 1) * rows, :] = jnp.full((rows, depth), bias_s[o], F32)
+        bias_v[o * rows:(o + 1) * rows, :] = jnp.full((rows, depth), 0.5 * bias_s[o], F32)
 
     def pointwise(x):
         grid = f_v[:, x].reshape(chans * rows, depth)
@@ -246,16 +251,19 @@
         return start + index * n_y + sender
 
     for c, members in enumerate(sets):
-        for d in members[::-1]:
-            for t in range(group - 1, -1, -1):
+        places = [(d, t) for d in members[::-1] for t in range(group - 1, -1, -1)]
+        for index in range(0, len(places), 4):
+            batch = places[index:index + 4]
+            sums = [[None, None] for _ in batch]
+            for j in range(first_share):
+                for h in range(2):
+                    mode = m_v[j, :, h * HALF:(h + 1) * HALF]
+                    for b, (d, t) in enumerate(batch):
+                        term = mode * sy_v[at(d, t), j:j + 1, :]
+                        sums[b][h] = term if j == 0 else sums[b][h] + term
+            for b, (d, t) in enumerate(batch):
                 target = at(d, t)
-                sides = []
-                for h in range(2):
-                    total = m_v[0, :, h * HALF:(h + 1) * HALF] * sy_v[target, 0:1, :]
-                    for j in range(1, first_share):
-                        total += m_v[j, :, h * HALF:(h + 1) * HALF] * sy_v[target, j:j + 1, :]
-                    sides.append(total)
-                tout[target] = jnp.concatenate(sides, axis=0).astype(BF16)
+                tout[target] = jnp.concatenate(sums[b], axis=0).astype(BF16)
                 for u in range(highs):
                     if d == 0 and t == 0 and u == 0:
                         landing[land(high, me_y)] = tout[target]
@@ -271,7 +279,8 @@
 
     for x in range(4, planes):
         pointwise(x)
-    loads[6].wait()
+    for load in loads[6:]:
+        load.wait()
 
     for c, members in enumerate(sets):
         count = len(members) * group * highs - (1 if 0 in members else 0)
@@ -295,11 +304,15 @@
                 device_id_type=MESH,
             ).start()
 
+    def turn(part_of, start):
+        value = modes[pl.ds(start, highs * planes)].astype(F32)
+        for h in range(2):
+            one = value[:, h * SHARE:(h + 1) * SHARE, :].reshape(side, HALF)
+            gt_out[h * HALF:(h + 1) * HALF, part_of * side:(part_of + 1) * side] = one.T.astype(BF16)
+
+    turn(0, low * highs * planes)
     arrived(modes.at[0:highs * planes], recv4)
-    for h in range(2):
-        value = modes[...].astype(F32)[:, h * SHARE:(h + 1) * SHARE, :]
-        value = value.reshape(planes * KZ, HALF)
-        gt_out[h * HALF:(h + 1) * HALF, :] = value.T.astype(BF16)
+    turn(1, (1 - low) * highs * planes)
     arrived(got1, send1)
     arrived(got2.at[0:len(others)], send2)
     arrived(got2.at[0:len(others)], send3)
@@ -313,9 +326,8 @@
     scale = math.sqrt(2.0 / math.pi)
     for x in range(planes):
         value = local[x] + jnp.dot(gt[...], synth[x], preferred_element_type=F32)
-        inner = value * (scale + (scale * 0.044715) * (value * value))
-        small = 0.5 * value
-        value = small + small * jnp.tanh(inner)
+        inner = value * (2.0 * scale + (8.0 * scale * 0.044715) * (value * value))
+        value += value * jnp.tanh(inner)
         o_v[:, x] = value.astype(BF16).reshape(chans, rows, depth)
         store = pltpu.make_async_copy(o_v.at[:, x], out.at[:, x], out_sem.at[x])
         store.start()
@@ -341,7 +353,7 @@
         out_shape=(
             pltpu.VMEM((planes, wide, depth), F32),
             pltpu.VMEM((wide, planes * KZ), BF16),
-            pltpu.VMEM(b_tab.shape[1:], BF16),
+            pltpu.VMEM((planes, planes * KZ, depth), BF16),
         ),
         in_specs=[hbm] * len(operands),
         out_specs=(vmem, vmem, vmem),
@@ -367,7 +379,7 @@
             pltpu.VMEM((n_y, 2 * SHARE, HALF), BF16),
             pltpu.VMEM((highs * n_y, 2 * SHARE, HALF), BF16),
             pltpu.VMEM((n_z * planes, 2 * SHARE, HALF), BF16),
-            dma((7,)),
+            dma((8,)),
             dma((planes,)),
             dma((planes,)),
             dma(()),

time: 23.8 us -> 23.6 us (level)
  no operation moved by 1% of the time
where the time goes in v4:
time: 23.6 us; the launch traced here: 23.5 us
  Pallas kernels  23.5 us (100%)
    pallas_call x1, Pallas kernels, shards(): pl.pallas_call(functools.partial(spectral_kernel, n_y, n_z), out_shape=(p...  21.2 us
    pallas_call x1, Pallas kernels, shards(): pl.pallas_call(grid_kernel, out_shape=jax.ShapeDtypeStruct(field.shape, B...  2.27 us

profile of v4, /device:TPU:1, one launch (start us, length us, event | category | flops | bytes accessed | tf_op | source)
XLA Modules:
  0.0 23.5 jit_solution(17291066240237167761)
XLA Ops:
  0.0 21.2 %spectral.1 = (f32[8,512,256]{2,1,0:T(8,128)S(1)}, bf16[512,256]{1,0:T(8,128)(2,1)S(1)}, bf16[8,256,256]{2,1,0:T(8,128)(2,1)S(1)}) custom-call(bf16[32,8,16,256]{3,2,1,0:T(8,128)(2,1)} %field.1, bf16[4,8,256,256]{3,2,1,0:T(8,128)(2,1)} %constant.8.clone.a_tab, bf16[4,8,2,128,256]{4,3,2,1,0:T(8,128)(2,1)} %constant.9.clone.b_tab, ...), custom_call_target="tpu_custom_call" | custom-call | tf_op jit(solution)/shard_map/spectral/pallas_call | solution.py:351
  21.2 2.3 %grid.1 = bf16[32,8,16,256]{3,2,1,0:T(8,128)(2,1)} custom-call(f32[8,512,256]{2,1,0:T(8,128)S(1)} %get-tuple-element.8.local, bf16[512,256]{1,0:T(8,128)(2,1)S(1)} %get-tuple-element.9.gt, bf16[8,256,256]{2,1,0:T(8,128)(2,1)S(1)} %get-tuple-element.10.synth), custom_call_target="tpu_custom_call" | custom-call | tf_op jit(solution)/shard_map/grid/pallas_call | solution.py:399

commit v5 on v4

--- a/solution.py
+++ b/solution.py
@@ -49,7 +49,8 @@
     analysis_y = lanes(ay)
     synth_y = np.ascontiguousarray(np.swapaxes(lanes(0.5 * sy), 1, 2))
     synth = joint(ax, sz).reshape(n_z, planes, 2, planes * KZ // 2, depth)
-    return joint(ax, az), synth, analysis_y, synth_y
+    analysis = np.ascontiguousarray(np.swapaxes(joint(ax, az), 2, 3))
+    return analysis, synth, analysis_y, synth_y
 
 
 def bits(count):
@@ -67,7 +68,7 @@
     n_y, n_z, field, a_tab, b_tab, weight, point, bias, ay_tab, sy_tab, local, gt_out, b_out,
     f_v, a_v, w_v, p_v, bias_s, bias_v, ay_v, sy_v, e1, e2, spread, kron,
     part, got1, owned, got2, u_v, m_v, tout, got3, modes,
-    load_sem, grid_sem, a_sem, send1, recv1, send2, recv2, send3, recv3, send4, recv4,
+    load_sem, send1, recv1, send2, recv2, send3, recv3, send4, recv4,
 ):
     me_y, me_z = lax.axis_index("gy"), lax.axis_index("gz")
     chans, planes, rows, depth = f_v.shape
@@ -109,27 +110,24 @@
             barrier, inc=1, device_id=(at(d, t), high_at(u) * 2 + low), device_id_type=MESH
         )
 
-    half = chans // 2
+    half = planes // 2
     side = planes * KZ // 2
-    grids = []
-    for x in range(planes):
-        one = pltpu.make_async_copy(a_tab.at[me_z, x], a_v.at[x], a_sem.at[x])
-        two = pltpu.make_async_copy(
-            field.at[0:half, x], f_v.at[0:half, x], grid_sem.at[x]
+    loads = []
+    for h in range(2):
+        of = pl.ds(h * half, half)
+        loads.append(pltpu.make_async_copy(a_tab.at[me_z, of], a_v.at[of], load_sem.at[2 * h]))
+        loads.append(
+            pltpu.make_async_copy(field.at[:, of], f_v.at[:, of], load_sem.at[2 * h + 1])
         )
-        one.start()
-        two.start()
-        grids.append((one, two))
-    loads = [
-        pltpu.make_async_copy(field.at[half:chans], f_v.at[half:chans], load_sem.at[0]),
-        pltpu.make_async_copy(point, p_v, load_sem.at[1]),
-        pltpu.make_async_copy(bias, bias_s, load_sem.at[2]),
-        pltpu.make_async_copy(weight, w_v, load_sem.at[3]),
-        pltpu.make_async_copy(ay_tab.at[block], ay_v, load_sem.at[4]),
-        pltpu.make_async_copy(sy_tab.at[block], sy_v, load_sem.at[5]),
-        pltpu.make_async_copy(b_tab.at[me_z, :, low], b_out.at[:, 0:side], load_sem.at[6]),
+    loads += [
+        pltpu.make_async_copy(weight, w_v, load_sem.at[4]),
+        pltpu.make_async_copy(point, p_v, load_sem.at[5]),
+        pltpu.make_async_copy(bias, bias_s, load_sem.at[6]),
+        pltpu.make_async_copy(ay_tab.at[block], ay_v, load_sem.at[7]),
+        pltpu.make_async_copy(sy_tab.at[block], sy_v, load_sem.at[8]),
+        pltpu.make_async_copy(b_tab.at[me_z, :, low], b_out.at[:, 0:side], load_sem.at[9]),
         pltpu.make_async_copy(
-            b_tab.at[me_z, :, 1 - low], b_out.at[:, side:2 * side], load_sem.at[7]
+            b_tab.at[me_z, :, 1 - low], b_out.at[:, side:2 * side], load_sem.at[10]
         ),
     ]
     for load in loads:
@@ -140,19 +138,20 @@
     ).astype(BF16)
 
     pair_order = range(pairs - 1, -1, -1)
+    total = None
     for h in range(2):
-        if h == 1:
-            loads[0].wait()
-        total = jnp.zeros((planes * KZ, HALF), F32)
-        for x in range(planes):
-            if h == 0:
-                for load in grids[x]:
-                    load.wait()
-            grid = f_v[h * half:(h + 1) * half, x].reshape(HALF, depth)
-            total += lax.dot_general(
-                a_v[x], grid, (((1,), (1,)), ((), ())), preferred_element_type=F32
-            )
-        part[h] = total.reshape(2, highs * pairs, 2 * SHARE, HALF).astype(BF16)
+        loads[2 * h].wait()
+        loads[2 * h + 1].wait()
+        planes_of = range(h * half, (h + 1) * half)
+        grid = jnp.concatenate(
+            [f_v[:, x].reshape(chans * rows, depth) for x in planes_of], axis=1
+        )
+        table = a_v[h * half:(h + 1) * half].reshape(half * depth, planes * KZ)
+        term = jnp.dot(grid, table, preferred_element_type=F32)
+        total = term if total is None else total + term
+    for h in range(2):
+        turned = total[h * HALF:(h + 1) * HALF].T
+        part[h] = turned.reshape(2, highs * pairs, 2 * SHARE, HALF).astype(BF16)
         if h == 0:
             pl.semaphore_wait(barrier, 1 + len(others))
         pltpu.make_async_remote_copy(
@@ -198,7 +197,7 @@
 
     spread[...] = select(spread.shape, lambda r: r >> bits(rows), lambda c: c).astype(BF16)
 
-    loads[1].wait()
+    loads[5].wait()
     wide = lax.dot_general(
         spread[...], p_v[...], (((1,), (1,)), ((), ())), preferred_element_type=F32
     ).astype(BF16)
@@ -207,7 +206,7 @@
     )
     same = select(wide.shape, lambda r: r & (rows - 1), lambda c: c & (rows - 1))
     kron[...] = (wide * (0.5 * same)).astype(BF16)
-    loads[2].wait()
+    loads[6].wait()
     for o in range(chans):
         bias_v[o * rows:(o + 1) * rows, :] = jnp.full((rows, depth), 0.5 * bias_s[o], F32)
 
@@ -219,7 +218,7 @@
     for x in range(4):
         pointwise(x)
 
-    for load in loads[3:6]:
+    for load in (loads[4], loads[7], loads[8]):
         load.wait()
     arrived(got2.at[0:len(others)], recv2)
     for h in range(2):
@@ -279,7 +278,7 @@
 
     for x in range(4, planes):
         pointwise(x)
-    for load in loads[6:]:
+    for load in loads[9:]:
         load.wait()
 
     for c, members in enumerate(sets):
@@ -379,9 +378,7 @@
             pltpu.VMEM((n_y, 2 * SHARE, HALF), BF16),
             pltpu.VMEM((highs * n_y, 2 * SHARE, HALF), BF16),
             pltpu.VMEM((n_z * planes, 2 * SHARE, HALF), BF16),
-            dma((8,)),
-            dma((planes,)),
-            dma((planes,)),
+            dma((11,)),
             dma(()),
             dma((2,)),
             dma(()),

time: 23.6 us -> 23.2 us (0.983)
  Pallas kernels: 23.5 us -> 23.1 us
    pallas_call x1, Pallas kernels: 21.2 us -> 20.8 us  [shards(): pl.pallas_call(functools.partial(spectral_kernel, n_y, n_z), out_shape=(p...]
where the time goes in v5:
time: 23.2 us; the launch traced here: 23.1 us
  Pallas kernels  23.1 us (100%)
    pallas_call x1, Pallas kernels, shards(): pl.pallas_call(functools.partial(spectral_kernel, n_y, n_z), out_shape=(p...  20.8 us
    pallas_call x1, Pallas kernels, shards(): pl.pallas_call(grid_kernel, out_shape=jax.ShapeDtypeStruct(field.shape, B...  2.27 us

profile of v5, /device:TPU:1, one launch (start us, length us, event | category | flops | bytes accessed | tf_op | source)
XLA Modules:
  0.0 23.1 jit_solution(11997085280647799050)
XLA Ops:
  0.0 20.8 %spectral.1 = (f32[8,512,256]{2,1,0:T(8,128)S(1)}, bf16[512,256]{1,0:T(8,128)(2,1)S(1)}, bf16[8,256,256]{2,1,0:T(8,128)(2,1)S(1)}) custom-call(bf16[32,8,16,256]{3,2,1,0:T(8,128)(2,1)} %field.1, bf16[4,8,256,256]{3,2,1,0:T(8,128)(2,1)} %constant.8.clone.a_tab, bf16[4,8,2,128,256]{4,3,2,1,0:T(8,128)(2,1)} %constant.9.clone.b_tab, ...), custom_call_target="tpu_custom_call" | custom-call | tf_op jit(solution)/shard_map/spectral/pallas_call | solution.py:350
  20.8 2.3 %grid.1 = bf16[32,8,16,256]{3,2,1,0:T(8,128)(2,1)} custom-call(f32[8,512,256]{2,1,0:T(8,128)S(1)} %get-tuple-element.8.local, bf16[512,256]{1,0:T(8,128)(2,1)S(1)} %get-tuple-element.9.gt, bf16[8,256,256]{2,1,0:T(8,128)(2,1)S(1)} %get-tuple-element.10.synth), custom_call_target="tpu_custom_call" | custom-call | tf_op jit(solution)/shard_map/grid/pallas_call | solution.py:396

commit v6 on v5

v6 whole, which is shorter than its diff:
```python
import functools
import math

import jax
import jax.numpy as jnp
import ml_dtypes
import numpy as np
from jax import lax
from jax.experimental import pallas as pl
from jax.experimental.pallas import tpu as pltpu
from jax.sharding import PartitionSpec as P

KY = 32
KZ = 32
BF16 = jnp.bfloat16
F32 = jnp.float32
MESH = pl.DeviceIdType.MESH
SHARE = 8
HALF = 256
LANES = 128


def basis(count, length, norm):
    modes = np.arange(count)[:, None]
    spots = np.arange(length)[None, :]
    value = norm * np.cos(np.pi * modes * (spots + 0.5) / length)
    return np.where(modes == 0, value * math.sqrt(0.5), value)


def tables(n_y, n_z, planes, rows, depth, first_share):
    total_rows, total_depth = rows * n_y, depth * n_z
    az = basis(KZ, total_depth, math.sqrt(2.0 / total_depth))
    az = az.astype(np.float32).astype(ml_dtypes.bfloat16).astype(np.float64)
    ax = basis(planes, planes, math.sqrt(2.0 / planes))
    sz = basis(KZ, total_depth, math.sqrt(2.0 / KZ))

    def joint(x_basis, z_basis):
        z = z_basis.reshape(n_z // 2, 2, SHARE, n_z, depth)
        both = np.einsum("ix,hlkdz->dxlhikz", x_basis, z)
        return both.reshape(n_z, planes, planes * KZ, depth).astype(ml_dtypes.bfloat16)

    ay = basis(KY, total_rows, math.sqrt(2.0 / total_rows))
    sy = basis(KY, total_rows, math.sqrt(2.0 / KY))
    blocks = KY // first_share

    def lanes(y_basis):
        parts = y_basis.reshape(blocks, first_share, n_y, rows)
        return np.tile(parts, (1, 1, 1, HALF // rows)).astype(np.float32)

    analysis_y = lanes(ay)
    synth_y = np.ascontiguousarray(np.swapaxes(lanes(0.5 * sy), 1, 2))
    synth = joint(ax, sz).reshape(n_z, planes, 2, planes * KZ // 2, depth)
    analysis = np.ascontiguousarray(np.swapaxes(joint(ax, az), 2, 3))
    return analysis, synth, analysis_y, synth_y


def bits(count):
    assert count & (count - 1) == 0
    return count.bit_length() - 1


def select(shape, row_of, column_of):
    r = row_of(lax.broadcasted_iota(jnp.int32, shape, 0))
    c = column_of(lax.broadcasted_iota(jnp.int32, shape, 1))
    return jnp.where(r == c, 1.0, 0.0).astype(F32)


def spectral_kernel(
    n_y, n_z, field, a_tab, b_tab, weight, point, bias, ay_tab, sy_tab, local, gt_out, b_out,
    f_v, a_v, w_v, p_v, bias_s, bias_v, ay_v, sy_v, e1, e2, spread, kron,
    part, got1, owned, got2, u_v, t_v, m_v, tout, got3, modes,
    load_sem, send1, recv1, send2, recv2, send3, recv3, send4, recv4,
):
    me_y, me_z = lax.axis_index("gy"), lax.axis_index("gz")
    chans, planes, rows, depth = f_v.shape
    group = n_y // planes
    highs = n_z // 2
    high, low = lax.div(me_z, 2), lax.rem(me_z, 2)
    near = high * 2 + 1 - low
    first_share = w_v.shape[0]
    mine, place = lax.div(me_y, group), lax.rem(me_y, group)
    block = place if first_share < KY else 0
    others = [
        (d, t, u) for d in range(planes) for t in range(group) for u in range(highs)
    ][1:]

    def flip(index, mask):
        for k in range(bits(planes)):
            if mask >> k & 1:
                bit = lax.rem(lax.div(index, 1 << k), 2)
                index = index + (1 << k) * (1 - 2 * bit)
        return index

    def at(d, t):
        return flip(mine, d) * group + lax.rem(place + t, group)

    def came(d, t):
        return flip(mine, d) * group + lax.rem(place - t + group, group)

    def high_at(u):
        return lax.rem(high + u, highs)

    def arrived(blocks, semaphore):
        pltpu.make_async_copy(blocks, blocks, semaphore).wait()

    barrier = pltpu.get_barrier_semaphore()
    pl.semaphore_signal(barrier, inc=1, device_id=(me_y, near), device_id_type=MESH)
    for d, t, u in others:
        pl.semaphore_signal(
            barrier, inc=1, device_id=(at(d, t), high_at(u) * 2 + low), device_id_type=MESH
        )

    half = chans // 2
    side = planes * KZ // 2
    loads = [
        pltpu.make_async_copy(a_tab.at[me_z], a_v, load_sem.at[0]),
        pltpu.make_async_copy(field.at[0:half], f_v.at[0:half], load_sem.at[1]),
        pltpu.make_async_copy(field.at[half:chans], f_v.at[half:chans], load_sem.at[2]),
        pltpu.make_async_copy(weight, w_v, load_sem.at[3]),
        pltpu.make_async_copy(point, p_v, load_sem.at[4]),
        pltpu.make_async_copy(bias, bias_s, load_sem.at[5]),
        pltpu.make_async_copy(ay_tab.at[block], ay_v, load_sem.at[6]),
        pltpu.make_async_copy(sy_tab.at[block], sy_v, load_sem.at[7]),
        pltpu.make_async_copy(b_tab.at[me_z, :, low], b_out.at[:, 0:side], load_sem.at[8]),
        pltpu.make_async_copy(
            b_tab.at[me_z, :, 1 - low], b_out.at[:, side:2 * side], load_sem.at[9]
        ),
    ]
    for load in loads:
        load.start()

    e1[...] = select(
        e1.shape, lambda r: r >> bits(rows), lambda c: c >> bits(chans)
    ).astype(BF16)

    def stacked(value):
        return jnp.concatenate([value[..., :LANES], value[..., LANES:]], axis=-2)

    table = a_v.reshape(planes * depth, planes * KZ)
    loads[0].wait()
    for h in range(2):
        loads[1 + h].wait()
        grid = jnp.concatenate(
            [f_v[h * half:(h + 1) * half, x].reshape(HALF, depth) for x in range(planes)], axis=1
        )
        turned = jnp.dot(grid, table[...], preferred_element_type=F32).T
        turned = turned.reshape(2, highs * planes, SHARE, HALF)
        part[h] = stacked(turned).astype(BF16)
        if h == 0:
            pl.semaphore_wait(barrier, 1 + len(others))
        pltpu.make_async_remote_copy(
            src_ref=part.at[h, 1 - low],
            dst_ref=got1.at[h],
            send_sem=send1,
            recv_sem=recv1.at[h],
            device_id=(me_y, near),
            device_id_type=MESH,
        ).start()

    for h in range(2):
        arrived(got1.at[h], recv1.at[h])
        owned[h] = (part[h, low].astype(F32) + got1[h].astype(F32)).astype(BF16)
        for d, t, u in others[::-1]:
            pltpu.make_async_remote_copy(
                src_ref=owned.at[h, high_at(u) * planes + flip(mine, d)],
                dst_ref=got2.at[h, high * n_y + me_y],
                send_sem=send2.at[h],
                recv_sem=recv2.at[h],
                device_id=(at(d, t), high_at(u) * 2 + low),
                device_id_type=MESH,
            ).start()
        got2[h, high * n_y + me_y] = owned[h, high * planes + mine]

    e2[...] = select(
        e2.shape, lambda r: r & (chans - 1), lambda c: c >> bits(rows)
    ).astype(BF16)
    spread[...] = select(spread.shape, lambda r: r >> bits(rows), lambda c: c).astype(BF16)

    loads[4].wait()
    wide = lax.dot_general(
        spread[...], p_v[...], (((1,), (1,)), ((), ())), preferred_element_type=F32
    ).astype(BF16)
    wide = lax.dot_general(
        wide, spread[...], (((1,), (1,)), ((), ())), preferred_element_type=F32
    )
    same = select(wide.shape, lambda r: r & (rows - 1), lambda c: c & (rows - 1))
    kron[...] = (wide * (0.5 * same)).astype(BF16)
    loads[5].wait()
    for o in range(chans):
        bias_v[o * rows:(o + 1) * rows, :] = jnp.full((rows, depth), 0.5 * bias_s[o], F32)

    def pointwise(x):
        grid = f_v[:, x].reshape(chans * rows, depth)
        value = jnp.dot(kron[...], grid, preferred_element_type=F32)
        local[x] = value + bias_v[...]

    for x in range(4):
        pointwise(x)

    for load in (loads[3], loads[6], loads[7]):
        load.wait()
    mode_rows = first_share * SHARE
    most = len(others)
    for h in range(2):
        arrived(got2.at[h, 0:most], recv2.at[h])
        pieces = []
        for s in range(n_y):
            total = got2[h, s].astype(F32)
            for u in range(1, highs):
                total += got2[h, u * n_y + s].astype(F32)
            pieces.append(total)
        for j in range(first_share):
            total = pieces[0] * ay_v[j, 0:1, :LANES]
            for s in range(1, n_y):
                total += pieces[s] * ay_v[j, s:s + 1, :LANES]
            u_v[h, j, :, :LANES] = total[:SHARE]
            u_v[h, j, :, LANES:] = total[SHARE:]
        spectrum = jnp.dot(
            u_v[h].reshape(mode_rows, HALF).astype(BF16), e1[...], preferred_element_type=F32
        )
        wide = half * chans
        weights = w_v[:, :, h * wide:(h + 1) * wide].astype(F32).reshape(mode_rows, wide)
        terms = spectrum * weights
        total = terms[:, :LANES]
        for lane in range(LANES, wide, LANES):
            total += terms[:, lane:lane + LANES]
        t_v[...] = total if h == 0 else t_v[...] + total

    landing = modes if group == 1 else got3

    def land(index, sender):
        start = low * highs * planes if group == 1 else 0
        return start + index * n_y + sender

    places = [(d, t) for d in range(planes) for t in range(group)][::-1]
    for g in range(2):
        mixed = jnp.dot(
            t_v[...].astype(BF16), e2[:, g * HALF:(g + 1) * HALF], preferred_element_type=F32
        )
        m_v[g] = mixed.reshape(first_share, SHARE, HALF)
        for index in range(0, len(places), 4):
            batch = places[index:index + 4]
            sums = [None] * len(batch)
            for j in range(first_share):
                mode = m_v[g, j]
                for b, (d, t) in enumerate(batch):
                    term = mode * sy_v[at(d, t), j:j + 1, :]
                    sums[b] = term if j == 0 else sums[b] + term
            for b, (d, t) in enumerate(batch):
                target = at(d, t)
                tout[g, target] = stacked(sums[b]).astype(BF16)
                for u in range(highs):
                    if d == 0 and t == 0 and u == 0:
                        landing[g, land(high, me_y)] = tout[g, target]
                        continue
                    pltpu.make_async_remote_copy(
                        src_ref=tout.at[g, target],
                        dst_ref=landing.at[g, land(high, me_y)],
                        send_sem=send3.at[g],
                        recv_sem=recv3.at[g],
                        device_id=(target, high_at(u) * 2 + low),
                        device_id_type=MESH,
                    ).start()

    for x in range(4, planes):
        pointwise(x)
    for load in loads[8:]:
        load.wait()

    block_of = pl.ds(low * highs * planes, highs * planes)
    for g in range(2):
        arrived(landing.at[g, 0:most], recv3.at[g])
        if group > 1:
            for index in range(highs):
                for i in range(planes):
                    total = got3[g, index * n_y + i * group].astype(F32)
                    for t in range(1, group):
                        total += got3[g, index * n_y + i * group + t].astype(F32)
                    modes[g, (low * highs + index) * planes + i] = total.astype(BF16)
        pltpu.make_async_remote_copy(
            src_ref=modes.at[g, block_of],
            dst_ref=modes.at[g, block_of],
            send_sem=send4.at[g],
            recv_sem=recv4.at[g],
            device_id=(me_y, near),
            device_id_type=MESH,
        ).start()

    def turn(g, part_of, start):
        value = modes[g, pl.ds(start, highs * planes)].astype(F32)
        for q in range(2):
            one = value[:, q * SHARE:(q + 1) * SHARE, :].reshape(side, LANES)
            first = g * HALF + q * LANES
            gt_out[first:first + LANES, part_of * side:(part_of + 1) * side] = one.T.astype(BF16)

    for g in range(2):
        turn(g, 0, low * highs * planes)
    for g in range(2):
        arrived(modes.at[g, 0:highs * planes], recv4.at[g])
        turn(g, 1, (1 - low) * highs * planes)
    arrived(got1, send1)
    for g in range(2):
        arrived(got2.at[g, 0:most], send2.at[g])
        arrived(got2.at[g, 0:most], send3.at[g])
        arrived(modes.at[g, 0:highs * planes], send4.at[g])


def grid_kernel(local, gt, synth, out, o_v, out_sem):
    planes, _, depth = local.shape
    chans, _, rows, _ = o_v.shape
    stores = []
    scale = math.sqrt(2.0 / math.pi)
    for x in range(planes):
        value = local[x] + jnp.dot(gt[...], synth[x], preferred_element_type=F32)
        inner = value * (2.0 * scale + (8.0 * scale * 0.044715) * (value * value))
        value += value * jnp.tanh(inner)
        o_v[:, x] = value.astype(BF16).reshape(chans, rows, depth)
        store = pltpu.make_async_copy(o_v.at[:, x], out.at[:, x], out_sem.at[x])
        store.start()
        stores.append(store)
    for store in stores:
        store.wait()


def shards(n_y, n_z, field, spectral_weight, point_weight, bias):
    chans, planes, rows, depth = field.shape
    first_share, depth_share = spectral_weight.shape[:2]
    assert depth_share == SHARE and chans * rows == 2 * HALF and first_share <= KY
    assert n_y % planes == 0 and depth_share * n_z == KZ and planes % 2 == 0 and n_z % 2 == 0
    a_tab, b_tab, ay_tab, sy_tab = tables(n_y, n_z, planes, rows, depth, first_share)
    highs = n_z // 2
    vmem = pl.BlockSpec(memory_space=pltpu.VMEM)
    hbm = pl.BlockSpec(memory_space=pltpu.HBM)
    wide = 2 * HALF
    dma = pltpu.SemaphoreType.DMA
    operands = [field, a_tab, b_tab, spectral_weight, point_weight, bias, ay_tab, sy_tab]
    local, gt, synth = pl.pallas_call(
        functools.partial(spectral_kernel, n_y, n_z),
        out_shape=(
            pltpu.VMEM((planes, wide, depth), F32),
            pltpu.VMEM((wide, planes * KZ), BF16),
            pltpu.VMEM((planes, planes * KZ, depth), BF16),
        ),
        in_specs=[hbm] * len(operands),
        out_specs=(vmem, vmem, vmem),
        scratch_shapes=[
            pltpu.VMEM(field.shape, BF16),
            pltpu.VMEM(a_tab.shape[1:], BF16),
            pltpu.VMEM(spectral_weight.shape, BF16),
            pltpu.VMEM(point_weight.shape, BF16),
            pltpu.SMEM(bias.shape, F32),
            pltpu.VMEM((wide, depth), F32),
            pltpu.VMEM(ay_tab.shape[1:], F32),
            pltpu.VMEM(sy_tab.shape[1:], F32),
            pltpu.VMEM((HALF, chans * chans // 2), BF16),
            pltpu.VMEM((LANES, wide), BF16),
            pltpu.VMEM((wide, chans), BF16),
            pltpu.VMEM((wide, wide), BF16),
            pltpu.VMEM((2, 2, highs * planes, 2 * SHARE, LANES), BF16),
            pltpu.VMEM((2, highs * planes, 2 * SHARE, LANES), BF16),
            pltpu.VMEM((2, highs * planes, 2 * SHARE, LANES), BF16),
            pltpu.VMEM((2, highs * n_y, 2 * SHARE, LANES), BF16),
            pltpu.VMEM((2, first_share, SHARE, HALF), F32),
            pltpu.VMEM((first_share * SHARE, LANES), F32),
            pltpu.VMEM((2, first_share, SHARE, HALF), F32),
            pltpu.VMEM((2, n_y, 2 * SHARE, LANES), BF16),
            pltpu.VMEM((2, highs * n_y, 2 * SHARE, LANES), BF16),
            pltpu.VMEM((2, 2 * highs * planes, 2 * SHARE, LANES), BF16),
            dma((10,)),
            dma(()),
            dma((2,)),
            dma((2,)),
            dma((2,)),
            dma((2,)),
            dma((2,)),
            dma((2,)),
            dma((2,)),
        ],
        compiler_params=pltpu.CompilerParams(
            collective_id=0, has_side_effects=True, vmem_limit_bytes=40 * 1024 * 1024
        ),
        name="spectral",
    )(*(pltpu.with_memory_space_constraint(value, pltpu.HBM) for value in operands))
    return pl.pallas_call(
        grid_kernel,
        out_shape=jax.ShapeDtypeStruct(field.shape, BF16),
        in_specs=[vmem] * 3,
        out_specs=hbm,
        scratch_shapes=[pltpu.VMEM(field.shape, BF16), dma((planes,))],
        compiler_params=pltpu.CompilerParams(vmem_limit_bytes=40 * 1024 * 1024),
        name="grid",
    )(local, gt, synth)


def solution(mesh):
    return jax.shard_map(
        functools.partial(shards, mesh.shape["gy"], mesh.shape["gz"]),
        mesh=mesh,
        in_specs=(P(None, None, "gy", "gz"), P("gy", "gz", None), P(), P()),
        out_specs=P(None, None, "gy", "gz"),
        check_vma=False,
    )
```

time: 23.2 us -> 22.7 us (0.978)
  Pallas kernels: 23.1 us -> 22.6 us
    pallas_call x1, Pallas kernels: 20.8 us -> 20.3 us  [shards(): pl.pallas_call(functools.partial(spectral_kernel, n_y, n_z), out_shape=(p...]
where the time goes in v6:
time: 22.7 us; the launch traced here: 22.6 us
  Pallas kernels  22.6 us (100%)
    pallas_call x1, Pallas kernels, shards(): pl.pallas_call(functools.partial(spectral_kernel, n_y, n_z), out_shape=(p...  20.3 us
    pallas_call x1, Pallas kernels, shards(): pl.pallas_call(grid_kernel, out_shape=jax.ShapeDtypeStruct(field.shape, B...  2.27 us

profile of v6, /device:TPU:1, one launch (start us, length us, event | category | flops | bytes accessed | tf_op | source)
XLA Modules:
  0.0 22.6 jit_solution(14437286119945335649)
XLA Ops:
  0.0 20.3 %spectral.1 = (f32[8,512,256]{2,1,0:T(8,128)S(1)}, bf16[512,256]{1,0:T(8,128)(2,1)S(1)}, bf16[8,256,256]{2,1,0:T(8,128)(2,1)S(1)}) custom-call(bf16[32,8,16,256]{3,2,1,0:T(8,128)(2,1)} %field.1, bf16[4,8,256,256]{3,2,1,0:T(8,128)(2,1)} %constant.8.clone.a_tab, bf16[4,8,2,128,256]{4,3,2,1,0:T(8,128)(2,1)} %constant.9.clone.b_tab, ...), custom_call_target="tpu_custom_call" | custom-call | tf_op jit(solution)/shard_map/spectral/pallas_call | solution.py:337
  20.3 2.3 %grid.1 = bf16[32,8,16,256]{3,2,1,0:T(8,128)(2,1)} custom-call(f32[8,512,256]{2,1,0:T(8,128)S(1)} %get-tuple-element.8.local, bf16[512,256]{1,0:T(8,128)(2,1)S(1)} %get-tuple-element.9.gt, bf16[8,256,256]{2,1,0:T(8,128)(2,1)S(1)} %get-tuple-element.10.synth), custom_call_target="tpu_custom_call" | custom-call | tf_op jit(solution)/shard_map/grid/pallas_call | solution.py:384

commit v7 on v6

--- a/solution.py
+++ b/solution.py
@@ -112,13 +112,15 @@
 
     half = chans // 2
     side = planes * KZ // 2
+    early = [
+        pltpu.make_async_copy(point, p_v, load_sem.at[4]),
+        pltpu.make_async_copy(bias, bias_s, load_sem.at[5]),
+    ]
     loads = [
         pltpu.make_async_copy(a_tab.at[me_z], a_v, load_sem.at[0]),
         pltpu.make_async_copy(field.at[0:half], f_v.at[0:half], load_sem.at[1]),
         pltpu.make_async_copy(field.at[half:chans], f_v.at[half:chans], load_sem.at[2]),
         pltpu.make_async_copy(weight, w_v, load_sem.at[3]),
-        pltpu.make_async_copy(point, p_v, load_sem.at[4]),
-        pltpu.make_async_copy(bias, bias_s, load_sem.at[5]),
         pltpu.make_async_copy(ay_tab.at[block], ay_v, load_sem.at[6]),
         pltpu.make_async_copy(sy_tab.at[block], sy_v, load_sem.at[7]),
         pltpu.make_async_copy(b_tab.at[me_z, :, low], b_out.at[:, 0:side], load_sem.at[8]),
@@ -126,12 +128,35 @@
             b_tab.at[me_z, :, 1 - low], b_out.at[:, side:2 * side], load_sem.at[9]
         ),
     ]
-    for load in loads:
+    for load in early + loads:
         load.start()
 
     e1[...] = select(
         e1.shape, lambda r: r >> bits(rows), lambda c: c >> bits(chans)
     ).astype(BF16)
+
+    e2[...] = select(
+        e2.shape, lambda r: r & (chans - 1), lambda c: c >> bits(rows)
+    ).astype(BF16)
+    spread[...] = select(spread.shape, lambda r: r >> bits(rows), lambda c: c).astype(BF16)
+
+    early[0].wait()
+    wide = lax.dot_general(
+        spread[...], p_v[...], (((1,), (1,)), ((), ())), preferred_element_type=F32
+    ).astype(BF16)
+    wide = lax.dot_general(
+        wide, spread[...], (((1,), (1,)), ((), ())), preferred_element_type=F32
+    )
+    same = select(wide.shape, lambda r: r & (rows - 1), lambda c: c & (rows - 1))
+    kron[...] = (wide * (0.5 * same)).astype(BF16)
+    early[1].wait()
+    for o in range(chans):
+        bias_v[o * rows:(o + 1) * rows, :] = jnp.full((rows, depth), 0.5 * bias_s[o], F32)
+
+    def pointwise(x):
+        grid = f_v[:, x].reshape(chans * rows, depth)
+        value = jnp.dot(kron[...], grid, preferred_element_type=F32)
+        local[x] = value + bias_v[...]
 
     def stacked(value):
         return jnp.concatenate([value[..., :LANES], value[..., LANES:]], axis=-2)
@@ -171,37 +196,16 @@
             ).start()
         got2[h, high * n_y + me_y] = owned[h, high * planes + mine]
 
-    e2[...] = select(
-        e2.shape, lambda r: r & (chans - 1), lambda c: c >> bits(rows)
-    ).astype(BF16)
-    spread[...] = select(spread.shape, lambda r: r >> bits(rows), lambda c: c).astype(BF16)
-
-    loads[4].wait()
-    wide = lax.dot_general(
-        spread[...], p_v[...], (((1,), (1,)), ((), ())), preferred_element_type=F32
-    ).astype(BF16)
-    wide = lax.dot_general(
-        wide, spread[...], (((1,), (1,)), ((), ())), preferred_element_type=F32
-    )
-    same = select(wide.shape, lambda r: r & (rows - 1), lambda c: c & (rows - 1))
-    kron[...] = (wide * (0.5 * same)).astype(BF16)
-    loads[5].wait()
-    for o in range(chans):
-        bias_v[o * rows:(o + 1) * rows, :] = jnp.full((rows, depth), 0.5 * bias_s[o], F32)
-
-    def pointwise(x):
-        grid = f_v[:, x].reshape(chans * rows, depth)
-        value = jnp.dot(kron[...], grid, preferred_element_type=F32)
-        local[x] = value + bias_v[...]
-
-    for x in range(4):
+    for x in range(3):
         pointwise(x)
 
-    for load in (loads[3], loads[6], loads[7]):
+    for load in loads[3:6]:
         load.wait()
     mode_rows = first_share * SHARE
     most = len(others)
     for h in range(2):
+        if h == 1:
+            pointwise(3)
         arrived(got2.at[h, 0:most], recv2.at[h])
         pieces = []
         for s in range(n_y):
@@ -262,13 +266,13 @@
                         device_id_type=MESH,
                     ).start()
 
-    for x in range(4, planes):
-        pointwise(x)
-    for load in loads[8:]:
+    for load in loads[6:]:
         load.wait()
 
     block_of = pl.ds(low * highs * planes, highs * planes)
     for g in range(2):
+        for x in range(4 + 2 * g, 6 + 2 * g):
+            pointwise(x)
         arrived(landing.at[g, 0:most], recv3.at[g])
         if group > 1:
             for index in range(highs):

time: 22.7 us -> 22.8 us (level)
  no operation moved by 1% of the time
where the time goes in v7:
time: 22.8 us; the launch traced here: 22.6 us
  Pallas kernels  22.6 us (99%)
    pallas_call x1, Pallas kernels, shards(): pl.pallas_call(functools.partial(spectral_kernel, n_y, n_z), out_shape=(p...  20.4 us
    pallas_call x1, Pallas kernels, shards(): pl.pallas_call(grid_kernel, out_shape=jax.ShapeDtypeStruct(field.shape, B...  2.27 us

profile of v7, /device:TPU:1, one launch (start us, length us, event | category | flops | bytes accessed | tf_op | source)
XLA Modules:
  0.0 22.6 jit_solution(9991065339049105380)
XLA Ops:
  0.0 20.4 %spectral.1 = (f32[8,512,256]{2,1,0:T(8,128)S(1)}, bf16[512,256]{1,0:T(8,128)(2,1)S(1)}, bf16[8,256,256]{2,1,0:T(8,128)(2,1)S(1)}) custom-call(bf16[32,8,16,256]{3,2,1,0:T(8,128)(2,1)} %field.1, bf16[4,8,256,256]{3,2,1,0:T(8,128)(2,1)} %constant.8.clone.a_tab, bf16[4,8,2,128,256]{4,3,2,1,0:T(8,128)(2,1)} %constant.9.clone.b_tab, ...), custom_call_target="tpu_custom_call" | custom-call | tf_op jit(solution)/shard_map/spectral/pallas_call | solution.py:341
  20.4 2.3 %grid.1 = bf16[32,8,16,256]{3,2,1,0:T(8,128)(2,1)} custom-call(f32[8,512,256]{2,1,0:T(8,128)S(1)} %get-tuple-element.8.local, bf16[512,256]{1,0:T(8,128)(2,1)S(1)} %get-tuple-element.9.gt, bf16[8,256,256]{2,1,0:T(8,128)(2,1)S(1)} %get-tuple-element.10.synth), custom_call_target="tpu_custom_call" | custom-call | tf_op jit(solution)/shard_map/grid/pallas_call | solution.py:388

commit v8 on v6

--- a/solution.py
+++ b/solution.py
@@ -103,13 +103,6 @@
     def arrived(blocks, semaphore):
         pltpu.make_async_copy(blocks, blocks, semaphore).wait()
 
-    barrier = pltpu.get_barrier_semaphore()
-    pl.semaphore_signal(barrier, inc=1, device_id=(me_y, near), device_id_type=MESH)
-    for d, t, u in others:
-        pl.semaphore_signal(
-            barrier, inc=1, device_id=(at(d, t), high_at(u) * 2 + low), device_id_type=MESH
-        )
-
     half = chans // 2
     side = planes * KZ // 2
     loads = [
@@ -128,6 +121,13 @@
     ]
     for load in loads:
         load.start()
+
+    barrier = pltpu.get_barrier_semaphore()
+    pl.semaphore_signal(barrier, inc=1, device_id=(me_y, near), device_id_type=MESH)
+    for d, t, u in others:
+        pl.semaphore_signal(
+            barrier, inc=1, device_id=(at(d, t), high_at(u) * 2 + low), device_id_type=MESH
+        )
 
     e1[...] = select(
         e1.shape, lambda r: r >> bits(rows), lambda c: c >> bits(chans)

time: 22.7 us -> 22.8 us (level)
  no operation moved by 1% of the time
where the time goes in v8:
time: 22.8 us; the launch traced here: 22.6 us
  Pallas kernels  22.6 us (99%)
    pallas_call x1, Pallas kernels, shards(): pl.pallas_call(functools.partial(spectral_kernel, n_y, n_z), out_shape=(p...  20.4 us
    pallas_call x1, Pallas kernels, shards(): pl.pallas_call(grid_kernel, out_shape=jax.ShapeDtypeStruct(field.shape, B...  2.27 us

profile of v8, /device:TPU:1, one launch (start us, length us, event | category | flops | bytes accessed | tf_op | source)
XLA Modules:
  0.0 22.6 jit_solution(8928608918745952097)
XLA Ops:
  0.0 20.4 %spectral.1 = (f32[8,512,256]{2,1,0:T(8,128)S(1)}, bf16[512,256]{1,0:T(8,128)(2,1)S(1)}, bf16[8,256,256]{2,1,0:T(8,128)(2,1)S(1)}) custom-call(bf16[32,8,16,256]{3,2,1,0:T(8,128)(2,1)} %field.1, bf16[4,8,256,256]{3,2,1,0:T(8,128)(2,1)} %constant.8.clone.a_tab, bf16[4,8,2,128,256]{4,3,2,1,0:T(8,128)(2,1)} %constant.9.clone.b_tab, ...), custom_call_target="tpu_custom_call" | custom-call | tf_op jit(solution)/shard_map/spectral/pallas_call | solution.py:337
  20.4 2.3 %grid.1 = bf16[32,8,16,256]{3,2,1,0:T(8,128)(2,1)} custom-call(f32[8,512,256]{2,1,0:T(8,128)S(1)} %get-tuple-element.8.local, bf16[512,256]{1,0:T(8,128)(2,1)S(1)} %get-tuple-element.9.gt, bf16[8,256,256]{2,1,0:T(8,128)(2,1)S(1)} %get-tuple-element.10.synth), custom_call_target="tpu_custom_call" | custom-call | tf_op jit(solution)/shard_map/grid/pallas_call | solution.py:384
